TPU v7x, 32 devices: a whole 2x2x4 slice. The times are simulated.
32 devices in a mesh: row: 8 (over z, y), col: 4 (over x, core).
Axes of the slice: x: 2, y: 2, z: 4, core: 2. Of those that a mesh axis runs over, the one named last changes fastest.
Arguments:
- vectors: bfloat16 [8, 4096], P(None, ('row', 'col')), may hold values from -6 to 6
- tiles: bfloat16 [8, 4, 32, 128, 128], P('row', 'col'), may hold values from -0.09375 to 0.09375
- tile_rows: int32 [8, 4, 32], P('row', 'col'), may hold values from 0 to 3, as said below
- tile_cols: int32 [8, 4, 32], P('row', 'col'), may hold values from 0 to 7, as said below
- tile_counts: int32 [8, 4], P('row', 'col'), may hold values from 1 to 32, as said below
Outputs:
- image: float32 [8, 4096], P(None, ('row', 'col'))
Inputs may be any that keep to these rules, and one draw needn't show every extreme that they name: A slot's tile lies on or below the diagonal: g * 4 + tile_rows >= tile_cols * 4 + h. A position may be named by several slots; their tiles add. tile_cols of grid row g are at most g. `tile_counts`: slots from the count on are padding. The grid position in the last grid row and first grid column uses all 32 slots.
All inputs are finite; a program needn't handle non-finite values.
Results may differ from a plain program's by a relative error of at most 0.0003.
Values may be sent and summed in bfloat16 or wider, within the bound.
No kernel may reach another device: no remote copies, remote signals or barrier semaphores. Data moves between devices by JAX's collectives and lax.ppermute only.
A program may use at most 64 MiB of HBM per device.

v0:
```python
import functools

import jax
import jax.numpy as jnp
from jax import lax
from jax.experimental import pallas as pl
from jax.experimental.pallas import tpu as pltpu
from jax.sharding import PartitionSpec as P

WHOLE = pl.BlockSpec(memory_space=pltpu.VMEM)
FAR = pl.BlockSpec(memory_space=pltpu.HBM)
SCALARS = pl.BlockSpec(memory_space=pltpu.SMEM)


def small_kernel(body, out_shape, in_specs, scratch_shapes=()):
    return pl.pallas_call(
        body,
        out_shape=out_shape,
        in_specs=in_specs,
        out_specs=[WHOLE] * len(out_shape),
        scratch_shapes=scratch_shapes,
        cost_estimate=pl.CostEstimate(flops=0, bytes_accessed=0, transcendentals=0),
        compiler_params=pltpu.CompilerParams(vmem_limit_bytes=4 << 20),
    )


def one_hots(places, targets, choice_ref, sums_ref):
    slots = places.shape[1]
    nvec = choice_ref.shape[0] // slots

    def iotas(shape):
        return [lax.broadcasted_iota(jnp.int32, shape, d) for d in (0, 1)]

    row, lane = iotas((nvec * slots, slots))
    mine = jnp.where(row // nvec == lane, places.astype(jnp.float32), 0.0)
    source = jnp.sum(mine, axis=1, keepdims=True).astype(jnp.int32)
    row, lane = iotas(choice_ref.shape)
    choice_ref[...] = jnp.where(
        (source == lane // nvec) & (row % nvec == lane % nvec), 1.0, 0.0
    ).astype(choice_ref.dtype)
    row, lane = iotas((slots, nvec * slots))
    spread = jnp.where(lane // nvec == row, 1.0, 0.0).astype(jnp.bfloat16)
    target = jnp.dot(
        jnp.broadcast_to(targets, (16, slots)).astype(jnp.bfloat16), spread, preferred_element_type=jnp.float32
    )[:1].astype(jnp.int32)
    row, lane = iotas(sums_ref.shape)
    sums_ref[...] = jnp.where(
        (row // nvec == target) & (row % nvec == lane % nvec), 1.0, 0.0
    ).astype(sums_ref.dtype)


def made_ready(rows_ref, cols_ref, vectors_ref, tiles_ref,
               col_choice, col_sums, row_choice, row_sums, own_ref, stored_ref, rows, cols, arrived):
    half = tiles_ref.shape[0] // 2
    loads = [
        pltpu.make_async_copy(rows_ref, rows, arrived.at[0]),
        pltpu.make_async_copy(cols_ref, cols, arrived.at[1]),
        pltpu.make_async_copy(vectors_ref, own_ref, arrived.at[2]),
    ] + [
        pltpu.make_async_copy(tiles_ref.at[pl.ds(k * half, half)], stored_ref.at[pl.ds(k * half, half)], arrived.at[3 + k])
        for k in range(2)
    ]
    for load in loads[:4]:
        load.start()
    loads[4].start(priority=1)
    for load in loads[:2]:
        load.wait()
    rows_axis, cols_axis = lax.axis_size("row"), lax.axis_size("col")
    far_rows = lax.axis_index("col") ^ rows[...]
    far_cols = lax.axis_index("row") ^ cols[...]
    crossed, bit = far_rows, 2
    while bit < cols_axis:
        crossed = crossed ^ ((far_rows & bit) // bit)
        bit *= 2
    spread = (far_cols & 2) * (rows_axis // 4) + (far_cols & 1) * (rows_axis // 4) + (far_cols >> 2)
    one_hots(crossed, spread, col_choice, col_sums)
    one_hots(far_cols, crossed, row_choice, row_sums)
    for load in loads[2:]:
        load.wait()


def slot_sums(contract, filled_ref, choice_ref, sums_ref, tiles_ref, *refs):
    *pieces, keep_ref, send_ref = refs
    nvec, width = keep_ref.shape[1:]
    stack = jnp.concatenate([p[...].astype(jnp.float32).reshape(-1, width) for p in pieces])
    x = jnp.dot(choice_ref[...], stack.astype(tiles_ref.dtype), preferred_element_type=jnp.float32)
    x = x.astype(tiles_ref.dtype)
    none = jnp.zeros((2 * nvec, width), x.dtype)
    high, low = [], []
    for first in range(0, tiles_ref.shape[0], 4):
        t = [tiles_ref[first + k] for k in range(4)]
        if contract == 1:
            t[1], t[2] = t[2], t[1]
        mine = x[first * nvec:(first + 4) * nvec]
        left = jnp.concatenate([mine[:2 * nvec], none])
        right = jnp.concatenate([none, mine[2 * nvec:]])
        block = jnp.concatenate([jnp.concatenate(t[:2], axis=1), jnp.concatenate(t[2:], axis=1)])
        found = lax.dot_general(
            jnp.concatenate([left, right], axis=1), block, (((1,), (contract,)), ((), ())),
            preferred_element_type=jnp.float32,
        )
        found = jnp.concatenate([
            found[k * nvec:(k + 1) * nvec, (k % 2) * width:(k % 2 + 1) * width] for k in range(4)
        ])
        high.append(found.astype(jnp.bfloat16))
        low.append((found - high[-1].astype(jnp.float32)).astype(jnp.bfloat16))
    both = jnp.concatenate([jnp.concatenate(high), jnp.concatenate(low)], axis=1)
    active = lax.broadcasted_iota(jnp.int32, sums_ref.shape, 1) < nvec * filled_ref[0, 0]
    sums = jnp.where(active, sums_ref[...].astype(jnp.float32), 0.0).astype(both.dtype)
    total = jnp.dot(sums, both, preferred_element_type=jnp.float32)
    total = (total[:, :width] + total[:, width:]).reshape(-1, nvec, width)
    half = keep_ref.shape[0]
    keep_ref[...] = total[:half]
    send_ref[...] = total[half:]


def joined(filled_ref, pair_ref, new_ref, out_ref):
    del filled_ref
    out_ref[0] = pair_ref[0]
    out_ref[1] = new_ref[1]
    out_ref[2] = pair_ref[1]
    out_ref[3] = new_ref[0]


def per_device(vectors, tiles, tile_rows, tile_cols, tile_counts):
    rows_axis = lax.axis_size("row")
    cols_axis = lax.axis_size("col")
    nvec, width = vectors.shape
    slots = tiles.shape[2]

    def swapped(x, axis, step):
        return lax.ppermute(x, axis, [(d, d ^ step) for d in range(lax.axis_size(axis))])

    def crossing(x, step):
        pairs = [(d, d ^ (step * cols_axis + 1)) for d in range(rows_axis * cols_axis)]
        return lax.ppermute(x, ("row", "col"), pairs)

    def far(x):
        return pltpu.with_memory_space_constraint(x, pltpu.HBM)

    def after(x, *earlier):
        return lax.optimization_barrier((x, *earlier))[0]

    def one_hot(rows, columns):
        return jax.ShapeDtypeStruct((rows * nvec, columns * nvec), jnp.bfloat16)

    def terms(contract, targets, choice, sums, pieces):
        half = jax.ShapeDtypeStruct((targets // 2, nvec, width), jnp.float32)
        return small_kernel(
            functools.partial(slot_sums, contract), [half, half], [SCALARS] + [WHOLE] * (3 + len(pieces))
        )(filled, choice, sums, stored, *pieces)

    near = swapped(vectors[None], "col", 1)
    col_choice, col_sums, row_choice, row_sums, own, stored = small_kernel(
        made_ready,
        [one_hot(slots, cols_axis), one_hot(rows_axis, slots), one_hot(slots, rows_axis), one_hot(cols_axis, slots)]
        + [jax.ShapeDtypeStruct(x.shape, x.dtype) for x in (vectors, tiles[0, 0])],
        [FAR] * 4,
        [pltpu.VMEM((1, slots), jnp.int32)] * 2 + [pltpu.SemaphoreType.DMA((5,))],
    )(*[far(x) for x in (tile_rows[0], tile_cols[0], vectors, tiles[0, 0])])
    own = own[None]
    pair = jnp.concatenate([own, near])
    row_new = crossing(pair, 1)
    col_stack = [pair]
    apart = 2
    while apart < cols_axis:
        col_stack.append(swapped(jnp.concatenate(col_stack), "col", apart + 1))
        apart *= 2
    filled = after(tile_counts, pair)
    mine, other = [own, row_new[1:]], [near, row_new[:1]]
    row_sent, = small_kernel(
        joined, [jax.ShapeDtypeStruct((4, nvec, width), vectors.dtype)], [SCALARS, WHOLE, WHOLE]
    )(filled, pair, row_new)
    row_new = crossing(row_sent, 2)
    col_stack[-1] = after(col_stack[-1], row_sent)
    col_keep, col_send = terms(0, rows_axis, col_choice, col_sums, col_stack)
    col_in = swapped(col_send, "row", 2)
    step = 2
    while 2 * step < rows_axis:
        row_new = after(row_new, col_send)
        mine.append(row_new[step:])
        other.append(row_new[:step])
        step *= 2
        row_sent = jnp.concatenate(other if 2 * step == rows_axis else mine + other)
        row_new = crossing(row_sent, step)
    col_terms = col_keep + after(col_in, row_sent)
    down = rows_axis // 4
    col_in = swapped(col_terms[down:], "row", 1)
    mine.append(after(row_new, col_terms))
    row_keep, row_send = terms(1, cols_axis, row_choice, row_sums, mine)
    across = cols_axis // 2
    row_in = swapped(row_send, "col", across + 1 if across > 1 else 1)
    col_in = after(col_in, row_keep)
    while down > 1:
        col_terms = col_terms[:down] + col_in
        down //= 2
        col_in = swapped(col_terms[down:], "row", 4 * down)
    row_terms = row_keep + after(row_in, col_terms[down:])
    while across > 1:
        across //= 2
        row_in = swapped(row_terms[across:], "col", across + 1 if across > 1 else 1)
        if across > 1:
            row_terms = row_terms[:across] + row_in
    return (row_terms[0] + row_in[0]) + (col_terms[0] + after(col_in, row_terms)[0])


def solution(mesh):
    return jax.shard_map(
        per_device,
        mesh=mesh,
        in_specs=(
            P(None, ("row", "col")),
            P("row", "col", None, None, None),
            P("row", "col", None),
            P("row", "col", None),
            P("row", "col"),
        ),
        out_specs=P(None, ("row", "col")),
        check_vma=False,
    )
```

profile of v0, /device:TPU:0, one launch (start us, length us, event | category | flops | bytes accessed | tf_op | source)
XLA Modules:
  0.0 21.1 jit_solution(1262367760537498919)
XLA Ops:
  0.0 0.5 %collective-permute-start = (bf16[1,8,128]{2,1,0:T(8,128)(2,1)}, bf16[1,8,128]{2,1,0:T(8,128)(2,1)S(1)}, u32[]{:S(2)}, u32[]{:S(2)}) collective-permute-start(bf16[1,8,128]{2,1,0:T(8,128)(2,1)} %bitcast.10), channel_id=1, source_target_pairs={{0,1},{1,0},{2,3},{3,2},{4,5},{5,4},{6,7},{7,6},{8,9},{9,8},{10,11... | collective-permute-start | bytes 6152 | tf_op jit(solution)/shard_map/ppermute | solution.py:132
  0.5 1.3 %shard_map.55 = (bf16[256,32]{1,0:T(8,128)(2,1)S(1)}, bf16[64,256]{1,0:T(8,128)(2,1)S(1)}, bf16[256,64]{1,0:T(8,128)(2,1)S(1)}, bf16[32,256]{1,0:T(8,128)(2,1)S(...) custom-call(s32[1,32]{1,0:T(1,128)} %bitcast.11, s32[1,32]{1,0:T(1,128)} %bitcast.12, ...), custom_call_target="tpu_custom_call" | custom-call | tf_op jit(solution)/shard_map/pallas_call | solution.py:154
  1.8 0.0 collective-permute-done
  1.8 2.7 %collective-permute-start.1 = (bf16[2,8,128]{2,1,0:T(8,128)(2,1)S(1)}, bf16[2,8,128]{2,1,0:T(8,128)(2,1)S(1)}, u32[]{:S(2)}, u32[]{:S(2)}) collective-permute-start(bf16[2,8,128]{2,1,0:T(8,128)(2,1)S(1)} %pad_maximum_fusion.1.pair_ref.refs_0_), channel_id=1, source_target_pairs={{0,5},{1,4},{2,7},{3,6},{4,1},{5,0},{6,3},{7,2},{8,13},{9,12},{10,... | collective-permute-start | bytes 12296 | tf_op jit(solution)/shard_map/ppermute | solution.py:136
  4.5 1.1 %collective-permute-start.3 = (bf16[2,8,128]{2,1,0:T(8,128)(2,1)S(1)}, bf16[2,8,128]{2,1,0:T(8,128)(2,1)S(1)}, u32[]{:S(2)}, u32[]{:S(2)}) collective-permute-start(bf16[2,8,128]{2,1,0:T(8,128)(2,1)S(1)} %pad_maximum_fusion.1.pair_ref.refs_0_), channel_id=1, source_target_pairs={{0,3},{1,2},{2,1},{3,0},{4,7},{5,6},{6,5},{7,4},{8,11},{9,10},{10,... | collective-permute-start | bytes 12296 | tf_op jit(solution)/shard_map/ppermute | solution.py:132
  6.2 0.0 collective-permute-done.1.new_ref
  6.2 1.8 %collective-permute-start.2 = (bf16[4,8,128]{2,1,0:T(8,128)(2,1)S(1)}, bf16[4,8,128]{2,1,0:T(8,128)(2,1)S(1)}, u32[]{:S(2)}, u32[]{:S(2)}) collective-permute-start(bf16[4,8,128]{2,1,0:T(8,128)(2,1)S(1)} %shard_map.56), channel_id=1, source_target_pairs={{0,9},{1,8},{2,11},{3,10},{4,13},{5,12},{6,15},{7,14},{8,1},{9,0},... | collective-permute-start | bytes 24584 | tf_op jit(solution)/shard_map/ppermute | solution.py:136
  8.0 0.0 collective-permute-done.3.refs_1_
  8.0 0.5 %shard_map.57 = (f32[4,8,128]{2,1,0:T(8,128)S(1)}, f32[4,8,128]{2,1,0:T(8,128)S(1)}) custom-call(s32[1,1]{1,0:T(1,128)S(6)} %copy.6.filled_ref, bf16[256,32]{1,0:T(8,128)(2,1)S(1)} %get-tuple-element.28.choice_ref, bf16[64,256]{1,0:T(8,128)(2,1)S(1)} %get-tuple-element.29.sums_ref, bf16[32,128,128]{2,1,0:T(8,128)(2,1)S(1)} %get-tuple-element.27.tiles_ref, ...), custom_call_target="tpu_custom_call" | custom-call | tf_op jit(solution)/shard_map/pallas_call | solution.py:149
  8.5 1.1 %collective-permute-start.5 = (f32[4,8,128]{2,1,0:T(8,128)S(1)}, f32[4,8,128]{2,1,0:T(8,128)S(1)}, u32[]{:S(2)}, u32[]{:S(2)}) collective-permute-start(f32[4,8,128]{2,1,0:T(8,128)S(1)} %get-tuple-element.31), channel_id=1, source_target_pairs={{0,8},{4,12},{8,0},{12,4},{16,24},{20,28},{24,16},{28,20},{1,9},{5... | collective-permute-start | bytes 49160 | tf_op jit(solution)/shard_map/ppermute | solution.py:132
  9.7 0.0 collective-permute-done.2
  9.7 2.5 %collective-permute-start.4 = (bf16[4,8,128]{2,1,0:T(8,128)(2,1)S(1)}, bf16[4,8,128]{2,1,0:T(8,128)(2,1)S(1)}, u32[]{:S(2)}, u32[]{:S(2)}) collective-permute-start(bf16[4,8,128]{2,1,0:T(8,128)(2,1)S(1)} %pad_maximum_fusion), channel_id=1, source_target_pairs={{0,17},{1,16},{2,19},{3,18},{4,21},{5,20},{6,23},{7,22},{8,25},{9,... | collective-permute-start | bytes 24584 | tf_op jit(solution)/shard_map/ppermute | solution.py:136
  12.2 0.2 collective-permute-done.5
  12.3 1.3 %collective-permute-start.7 = (f32[2,8,128]{2,1,0:T(8,128)S(1)}, f32[2,8,128]{2,1,0:T(8,128)S(1)}, u32[]{:S(2)}, u32[]{:S(2)}) collective-permute-start(f32[2,8,128]{2,1,0:T(8,128)S(1)} %slice.44), channel_id=1, source_target_pairs={{0,4},{4,0},{8,12},{12,8},{16,20},{20,16},{24,28},{28,24},{1,5},{5... | collective-permute-start | bytes 24584 | tf_op jit(solution)/shard_map/ppermute | solution.py:132
  13.7 0.1 collective-permute-done.4.refs_3_
  13.7 0.6 %shard_map.58 = (f32[2,8,128]{2,1,0:T(8,128)S(1)}, f32[2,8,128]{2,1,0:T(8,128)S(1)}) custom-call(s32[1,1]{1,0:T(1,128)S(6)} %copy.6.filled_ref, bf16[256,64]{1,0:T(8,128)(2,1)S(1)} %get-tuple-element.25.choice_ref, bf16[32,256]{1,0:T(8,128)(2,1)S(1)} %get-tuple-element.26.sums_ref, bf16[32,128,128]{2,1,0:T(8,128)(2,1)S(1)} %get-tuple-element.27.tiles_ref, ...), custom_call_target="tpu_custom_call" | custom-call | tf_op jit(solution)/shard_map/pallas_call | solution.py:149
  14.3 1.2 %collective-permute-start.6 = (f32[2,8,128]{2,1,0:T(8,128)S(1)}, f32[2,8,128]{2,1,0:T(8,128)S(1)}, u32[]{:S(2)}, u32[]{:S(2)}) collective-permute-start(f32[2,8,128]{2,1,0:T(8,128)S(1)} %get-tuple-element.37), channel_id=1, source_target_pairs={{0,3},{1,2},{2,1},{3,0},{4,7},{5,6},{6,5},{7,4},{8,11},{9,10},{10,... | collective-permute-start | bytes 24584 | tf_op jit(solution)/shard_map/ppermute | solution.py:132
  15.5 0.5 %collective-permute-done.7 = f32[2,8,128]{2,1,0:T(8,128)S(1)} collective-permute-done((f32[2,8,128]{2,1,0:T(8,128)S(1)}, f32[2,8,128]{2,1,0:T(8,128)S(1)}, u32[]{:S(2)}, u32[]{:S(2)}) %collective-permute-start.7) | collective-permute-done | bytes 8224 | tf_op jit(solution)/shard_map/ppermute | solution.py:132
  16.0 2.6 %collective-permute-start.9 = (f32[1,8,128]{2,1,0:T(8,128)S(1)}, f32[1,8,128]{2,1,0:T(8,128)S(1)}, u32[]{:S(2)}, u32[]{:S(2)}) collective-permute-start(f32[1,8,128]{2,1,0:T(8,128)S(1)} %slice.45), channel_id=1, source_target_pairs={{0,16},{4,20},{8,24},{12,28},{16,0},{20,4},{24,8},{28,12},{1,17},{... | collective-permute-start | bytes 12296 | tf_op jit(solution)/shard_map/ppermute | solution.py:132
  18.6 0.0 collective-permute-done.6
  18.6 0.1 collective-permute-start.8
  18.7 1.8 %collective-permute-done.9 = f32[1,8,128]{2,1,0:T(8,128)S(1)} collective-permute-done((f32[1,8,128]{2,1,0:T(8,128)S(1)}, f32[1,8,128]{2,1,0:T(8,128)S(1)}, u32[]{:S(2)}, u32[]{:S(2)}) %collective-permute-start.9) | collective-permute-done | bytes 4128 | tf_op jit(solution)/shard_map/ppermute | solution.py:132
  20.5 0.0 collective-permute-done.8
  20.5 0.6 %fusion.1 = f32[8,128]{1,0:T(8,128)} fusion(f32[1,8,128]{2,1,0:T(8,128)S(1)} %collective-permute-done.9, f32[2,8,128]{2,1,0:T(8,128)S(1)} %slice_add_fusion, f32[1,8,128]{2,1,0:T(8,128)S(1)} %collective-permute-done.8, f32[2,8,128]{2,1,0:T(8,128)S(1)} %add.25), kind=kLoop, calls=%fused_computation.4 | loop fusion | flops 3072 | bytes 20480 | tf_op jit(solution)/shard_map/add | solution.py:204
  (11 shorter events, 0.0 us)
Async XLA Ops:
  0.0 1.8 %collective-permute-start = (bf16[1,8,128]{2,1,0:T(8,128)(2,1)}, bf16[1,8,128]{2,1,0:T(8,128)(2,1)S(1)}, u32[]{:S(2)}, u32[]{:S(2)}) collective-permute-start(bf16[1,8,128]{2,1,0:T(8,128)(2,1)} %bitcast.10), channel_id=1, source_target_pairs={{0,1},{1,0},{2,3},{3,2},{4,5},{5,4},{6,7},{7,6},{8,9},{9,8},{10,11... | collective-permute-start | bytes 6152 | tf_op jit(solution)/shard_map/ppermute | solution.py:132
  1.8 4.4 %collective-permute-start.1 = (bf16[2,8,128]{2,1,0:T(8,128)(2,1)S(1)}, bf16[2,8,128]{2,1,0:T(8,128)(2,1)S(1)}, u32[]{:S(2)}, u32[]{:S(2)}) collective-permute-start(bf16[2,8,128]{2,1,0:T(8,128)(2,1)S(1)} %pad_maximum_fusion.1.pair_ref.refs_0_), channel_id=1, source_target_pairs={{0,5},{1,4},{2,7},{3,6},{4,1},{5,0},{6,3},{7,2},{8,13},{9,12},{10,... | collective-permute-start | bytes 12296 | tf_op jit(solution)/shard_map/ppermute | solution.py:136
  4.5 3.5 %collective-permute-start.3 = (bf16[2,8,128]{2,1,0:T(8,128)(2,1)S(1)}, bf16[2,8,128]{2,1,0:T(8,128)(2,1)S(1)}, u32[]{:S(2)}, u32[]{:S(2)}) collective-permute-start(bf16[2,8,128]{2,1,0:T(8,128)(2,1)S(1)} %pad_maximum_fusion.1.pair_ref.refs_0_), channel_id=1, source_target_pairs={{0,3},{1,2},{2,1},{3,0},{4,7},{5,6},{6,5},{7,4},{8,11},{9,10},{10,... | collective-permute-start | bytes 12296 | tf_op jit(solution)/shard_map/ppermute | solution.py:132
  6.2 3.4 %collective-permute-start.2 = (bf16[4,8,128]{2,1,0:T(8,128)(2,1)S(1)}, bf16[4,8,128]{2,1,0:T(8,128)(2,1)S(1)}, u32[]{:S(2)}, u32[]{:S(2)}) collective-permute-start(bf16[4,8,128]{2,1,0:T(8,128)(2,1)S(1)} %shard_map.56), channel_id=1, source_target_pairs={{0,9},{1,8},{2,11},{3,10},{4,13},{5,12},{6,15},{7,14},{8,1},{9,0},... | collective-permute-start | bytes 24584 | tf_op jit(solution)/shard_map/ppermute | solution.py:136
  8.5 3.8 %collective-permute-start.5 = (f32[4,8,128]{2,1,0:T(8,128)S(1)}, f32[4,8,128]{2,1,0:T(8,128)S(1)}, u32[]{:S(2)}, u32[]{:S(2)}) collective-permute-start(f32[4,8,128]{2,1,0:T(8,128)S(1)} %get-tuple-element.31), channel_id=1, source_target_pairs={{0,8},{4,12},{8,0},{12,4},{16,24},{20,28},{24,16},{28,20},{1,9},{5... | collective-permute-start | bytes 49160 | tf_op jit(solution)/shard_map/ppermute | solution.py:132
  9.7 4.0 %collective-permute-start.4 = (bf16[4,8,128]{2,1,0:T(8,128)(2,1)S(1)}, bf16[4,8,128]{2,1,0:T(8,128)(2,1)S(1)}, u32[]{:S(2)}, u32[]{:S(2)}) collective-permute-start(bf16[4,8,128]{2,1,0:T(8,128)(2,1)S(1)} %pad_maximum_fusion), channel_id=1, source_target_pairs={{0,17},{1,16},{2,19},{3,18},{4,21},{5,20},{6,23},{7,22},{8,25},{9,... | collective-permute-start | bytes 24584 | tf_op jit(solution)/shard_map/ppermute | solution.py:136
  12.3 3.7 %collective-permute-start.7 = (f32[2,8,128]{2,1,0:T(8,128)S(1)}, f32[2,8,128]{2,1,0:T(8,128)S(1)}, u32[]{:S(2)}, u32[]{:S(2)}) collective-permute-start(f32[2,8,128]{2,1,0:T(8,128)S(1)} %slice.44), channel_id=1, source_target_pairs={{0,4},{4,0},{8,12},{12,8},{16,20},{20,16},{24,28},{28,24},{1,5},{5... | collective-permute-start | bytes 24584 | tf_op jit(solution)/shard_map/ppermute | solution.py:132
  14.3 4.3 %collective-permute-start.6 = (f32[2,8,128]{2,1,0:T(8,128)S(1)}, f32[2,8,128]{2,1,0:T(8,128)S(1)}, u32[]{:S(2)}, u32[]{:S(2)}) collective-permute-start(f32[2,8,128]{2,1,0:T(8,128)S(1)} %get-tuple-element.37), channel_id=1, source_target_pairs={{0,3},{1,2},{2,1},{3,0},{4,7},{5,6},{6,5},{7,4},{8,11},{9,10},{10,... | collective-permute-start | bytes 24584 | tf_op jit(solution)/shard_map/ppermute | solution.py:132
  16.0 4.5 %collective-permute-start.9 = (f32[1,8,128]{2,1,0:T(8,128)S(1)}, f32[1,8,128]{2,1,0:T(8,128)S(1)}, u32[]{:S(2)}, u32[]{:S(2)}) collective-permute-start(f32[1,8,128]{2,1,0:T(8,128)S(1)} %slice.45), channel_id=1, source_target_pairs={{0,16},{4,20},{8,24},{12,28},{16,0},{20,4},{24,8},{28,12},{1,17},{... | collective-permute-start | bytes 12296 | tf_op jit(solution)/shard_map/ppermute | solution.py:132
  18.6 1.9 %collective-permute-start.8 = (f32[1,8,128]{2,1,0:T(8,128)S(1)}, f32[1,8,128]{2,1,0:T(8,128)S(1)}, u32[]{:S(2)}, u32[]{:S(2)}) collective-permute-start(f32[1,8,128]{2,1,0:T(8,128)S(1)} %slice.47), channel_id=1, source_target_pairs={{0,1},{1,0},{2,3},{3,2},{4,5},{5,4},{6,7},{7,6},{8,9},{9,8},{10,11... | collective-permute-start | bytes 12296 | tf_op jit(solution)/shard_map/ppermute | solution.py:132
where the time goes:
time: 21.3 us; the launch traced here: 21.1 us
  starting transfers between devices  14.8 us (69%)
  waiting for transfers between devices  2.55 us (12%)
  Pallas kernels  2.39 us (11%)
  between operations  0.72 us (3%)
  other arithmetic  0.62 us (3%)
    ppermute x7, starting transfers between devices, swapped(): lax.ppermute(x, axis, [(d, d ^ step) for d in range(lax.axis_size(axis))])  7.89 us
    ppermute x3, starting transfers between devices, crossing(): return lax.ppermute(x, ('row', 'col'), pairs)  6.93 us
    ppermute x7, waiting for transfers between devices, swapped(): lax.ppermute(x, axis, [(d, d ^ step) for d in range(lax.axis_size(axis))])  2.49 us
    pallas_call x1, Pallas kernels, per_device(): small_kernel(made_ready, [one_hot(slots, cols_axis), one_hot(rows_axis, s...  1.29 us
    pallas_call x2, Pallas kernels, terms(): small_kernel(functools.partial(slot_sums, contract), [half, half], [SCALA...  1.1 us
    add x1, other arithmetic, per_device(): row_terms[0] + row_in[0] + (col_terms[0] + after(col_in, row_terms)[0])  0.6 us
  transfers between devices with their start and end apart: 10, of which 4 were waited for; matrix products, arithmetic and copies ran while one was open for 0% of the time, Pallas kernels for 11%

commit v1 on v0

--- a/solution.py
+++ b/solution.py
@@ -74,7 +74,8 @@
         bit *= 2
     spread = (far_cols & 2) * (rows_axis // 4) + (far_cols & 1) * (rows_axis // 4) + (far_cols >> 2)
     one_hots(crossed, spread, col_choice, col_sums)
-    one_hots(far_cols, crossed, row_choice, row_sums)
+    order = (far_cols & 1) * 2 + (far_cols & 2) // 2 + (far_cols >> 2) * 4
+    one_hots(order, crossed, row_choice, row_sums)
     for load in loads[2:]:
         load.wait()
 
@@ -160,7 +161,7 @@
     )(*[far(x) for x in (tile_rows[0], tile_cols[0], vectors, tiles[0, 0])])
     own = own[None]
     pair = jnp.concatenate([own, near])
-    row_new = crossing(pair, 1)
+    row_new = crossing(pair, 2)
     col_stack = [pair]
     apart = 2
     while apart < cols_axis:
@@ -171,7 +172,7 @@
     row_sent, = small_kernel(
         joined, [jax.ShapeDtypeStruct((4, nvec, width), vectors.dtype)], [SCALARS, WHOLE, WHOLE]
     )(filled, pair, row_new)
-    row_new = crossing(row_sent, 2)
+    row_new = crossing(row_sent, 1)
     col_stack[-1] = after(col_stack[-1], row_sent)
     col_keep, col_send = terms(0, rows_axis, col_choice, col_sums, col_stack)
     col_in = swapped(col_send, "row", 2)

time: 21.3 us -> 21.3 us (level)
  starting transfers between devices: 14.8 us -> 15.1 us
  waiting for transfers between devices: 2.55 us -> 2.3 us
    ppermute x7, starting transfers between devices: 7.89 us -> 8.27 us  [swapped(): lax.ppermute(x, axis, [(d, d ^ step) for d in range(lax.axis_size(axis))])]
    ppermute x7, waiting for transfers between devices: 2.49 us -> 2.21 us  [swapped(): lax.ppermute(x, axis, [(d, d ^ step) for d in range(lax.axis_size(axis))])]
where the time goes in v1:
time: 21.3 us; the launch traced here: 21.1 us
  starting transfers between devices  15.1 us (71%)
  Pallas kernels  2.39 us (11%)
  waiting for transfers between devices  2.3 us (11%)
  between operations  0.72 us (3%)
  other arithmetic  0.62 us (3%)
    ppermute x7, starting transfers between devices, swapped(): lax.ppermute(x, axis, [(d, d ^ step) for d in range(lax.axis_size(axis))])  8.27 us
    ppermute x3, starting transfers between devices, crossing(): return lax.ppermute(x, ('row', 'col'), pairs)  6.81 us
    ppermute x7, waiting for transfers between devices, swapped(): lax.ppermute(x, axis, [(d, d ^ step) for d in range(lax.axis_size(axis))])  2.21 us
    pallas_call x1, Pallas kernels, per_device(): small_kernel(made_ready, [one_hot(slots, cols_axis), one_hot(rows_axis, s...  1.29 us
    pallas_call x2, Pallas kernels, terms(): small_kernel(functools.partial(slot_sums, contract), [half, half], [SCALA...  1.1 us
    add x1, other arithmetic, per_device(): row_terms[0] + row_in[0] + (col_terms[0] + after(col_in, row_terms)[0])  0.6 us
  transfers between devices with their start and end apart: 10, of which 4 were waited for; matrix products, arithmetic and copies ran while one was open for 0% of the time, Pallas kernels for 11%

profile of v1, /device:TPU:0, one launch (start us, length us, event | category | flops | bytes accessed | tf_op | source)
XLA Modules:
  0.0 21.1 jit_solution(17184302654691562642)
XLA Ops:
  0.0 0.5 %collective-permute-start = (bf16[1,8,128]{2,1,0:T(8,128)(2,1)}, bf16[1,8,128]{2,1,0:T(8,128)(2,1)S(1)}, u32[]{:S(2)}, u32[]{:S(2)}) collective-permute-start(bf16[1,8,128]{2,1,0:T(8,128)(2,1)} %bitcast.10), channel_id=1, source_target_pairs={{0,1},{1,0},{2,3},{3,2},{4,5},{5,4},{6,7},{7,6},{8,9},{9,8},{10,11... | collective-permute-start | bytes 6152 | tf_op jit(solution)/shard_map/ppermute | solution.py:133
  0.5 1.3 %shard_map.55 = (bf16[256,32]{1,0:T(8,128)(2,1)S(1)}, bf16[64,256]{1,0:T(8,128)(2,1)S(1)}, bf16[256,64]{1,0:T(8,128)(2,1)S(1)}, bf16[32,256]{1,0:T(8,128)(2,1)S(...) custom-call(s32[1,32]{1,0:T(1,128)} %bitcast.11, s32[1,32]{1,0:T(1,128)} %bitcast.12, ...), custom_call_target="tpu_custom_call" | custom-call | tf_op jit(solution)/shard_map/pallas_call | solution.py:155
  1.8 0.0 collective-permute-done
  1.8 2.8 %collective-permute-start.1 = (bf16[2,8,128]{2,1,0:T(8,128)(2,1)S(1)}, bf16[2,8,128]{2,1,0:T(8,128)(2,1)S(1)}, u32[]{:S(2)}, u32[]{:S(2)}) collective-permute-start(bf16[2,8,128]{2,1,0:T(8,128)(2,1)S(1)} %pad_maximum_fusion.1.pair_ref.refs_0_), channel_id=1, source_target_pairs={{0,9},{1,8},{2,11},{3,10},{4,13},{5,12},{6,15},{7,14},{8,1},{9,0},... | collective-permute-start | bytes 12296 | tf_op jit(solution)/shard_map/ppermute | solution.py:137
  4.5 1.1 %collective-permute-start.3 = (bf16[2,8,128]{2,1,0:T(8,128)(2,1)S(1)}, bf16[2,8,128]{2,1,0:T(8,128)(2,1)S(1)}, u32[]{:S(2)}, u32[]{:S(2)}) collective-permute-start(bf16[2,8,128]{2,1,0:T(8,128)(2,1)S(1)} %pad_maximum_fusion.1.pair_ref.refs_0_), channel_id=1, source_target_pairs={{0,3},{1,2},{2,1},{3,0},{4,7},{5,6},{6,5},{7,4},{8,11},{9,10},{10,... | collective-permute-start | bytes 12296 | tf_op jit(solution)/shard_map/ppermute | solution.py:133
  6.3 0.0 collective-permute-done.1.new_ref
  6.3 1.7 %collective-permute-start.2 = (bf16[4,8,128]{2,1,0:T(8,128)(2,1)S(1)}, bf16[4,8,128]{2,1,0:T(8,128)(2,1)S(1)}, u32[]{:S(2)}, u32[]{:S(2)}) collective-permute-start(bf16[4,8,128]{2,1,0:T(8,128)(2,1)S(1)} %shard_map.56), channel_id=1, source_target_pairs={{0,5},{1,4},{2,7},{3,6},{4,1},{5,0},{6,3},{7,2},{8,13},{9,12},{10,... | collective-permute-start | bytes 24584 | tf_op jit(solution)/shard_map/ppermute | solution.py:137
  8.0 0.0 collective-permute-done.3.refs_1_
  8.0 0.5 %shard_map.57 = (f32[4,8,128]{2,1,0:T(8,128)S(1)}, f32[4,8,128]{2,1,0:T(8,128)S(1)}) custom-call(s32[1,1]{1,0:T(1,128)S(6)} %copy.6.filled_ref, bf16[256,32]{1,0:T(8,128)(2,1)S(1)} %get-tuple-element.28.choice_ref, bf16[64,256]{1,0:T(8,128)(2,1)S(1)} %get-tuple-element.29.sums_ref, bf16[32,128,128]{2,1,0:T(8,128)(2,1)S(1)} %get-tuple-element.27.tiles_ref, ...), custom_call_target="tpu_custom_call" | custom-call | tf_op jit(solution)/shard_map/pallas_call | solution.py:150
  8.5 1.3 %collective-permute-start.5 = (f32[4,8,128]{2,1,0:T(8,128)S(1)}, f32[4,8,128]{2,1,0:T(8,128)S(1)}, u32[]{:S(2)}, u32[]{:S(2)}) collective-permute-start(f32[4,8,128]{2,1,0:T(8,128)S(1)} %get-tuple-element.31), channel_id=1, source_target_pairs={{0,8},{4,12},{8,0},{12,4},{16,24},{20,28},{24,16},{28,20},{1,9},{5... | collective-permute-start | bytes 49160 | tf_op jit(solution)/shard_map/ppermute | solution.py:133
  9.8 0.0 collective-permute-done.2
  9.9 2.4 %collective-permute-start.4 = (bf16[4,8,128]{2,1,0:T(8,128)(2,1)S(1)}, bf16[4,8,128]{2,1,0:T(8,128)(2,1)S(1)}, u32[]{:S(2)}, u32[]{:S(2)}) collective-permute-start(bf16[4,8,128]{2,1,0:T(8,128)(2,1)S(1)} %pad_maximum_fusion), channel_id=1, source_target_pairs={{0,17},{1,16},{2,19},{3,18},{4,21},{5,20},{6,23},{7,22},{8,25},{9,... | collective-permute-start | bytes 24584 | tf_op jit(solution)/shard_map/ppermute | solution.py:137
  12.2 0.1 collective-permute-done.5
  12.3 1.5 %collective-permute-start.7 = (f32[2,8,128]{2,1,0:T(8,128)S(1)}, f32[2,8,128]{2,1,0:T(8,128)S(1)}, u32[]{:S(2)}, u32[]{:S(2)}) collective-permute-start(f32[2,8,128]{2,1,0:T(8,128)S(1)} %slice.44), channel_id=1, source_target_pairs={{0,4},{4,0},{8,12},{12,8},{16,20},{20,16},{24,28},{28,24},{1,5},{5... | collective-permute-start | bytes 24584 | tf_op jit(solution)/shard_map/ppermute | solution.py:133
  13.8 0.1 collective-permute-done.4.refs_3_
  13.9 0.6 %shard_map.58 = (f32[2,8,128]{2,1,0:T(8,128)S(1)}, f32[2,8,128]{2,1,0:T(8,128)S(1)}) custom-call(s32[1,1]{1,0:T(1,128)S(6)} %copy.6.filled_ref, bf16[256,64]{1,0:T(8,128)(2,1)S(1)} %get-tuple-element.25.choice_ref, bf16[32,256]{1,0:T(8,128)(2,1)S(1)} %get-tuple-element.26.sums_ref, bf16[32,128,128]{2,1,0:T(8,128)(2,1)S(1)} %get-tuple-element.27.tiles_ref, ...), custom_call_target="tpu_custom_call" | custom-call | tf_op jit(solution)/shard_map/pallas_call | solution.py:150
  14.5 1.2 %collective-permute-start.6 = (f32[2,8,128]{2,1,0:T(8,128)S(1)}, f32[2,8,128]{2,1,0:T(8,128)S(1)}, u32[]{:S(2)}, u32[]{:S(2)}) collective-permute-start(f32[2,8,128]{2,1,0:T(8,128)S(1)} %get-tuple-element.37), channel_id=1, source_target_pairs={{0,3},{1,2},{2,1},{3,0},{4,7},{5,6},{6,5},{7,4},{8,11},{9,10},{10,... | collective-permute-start | bytes 24584 | tf_op jit(solution)/shard_map/ppermute | solution.py:133
  15.7 0.3 %collective-permute-done.7 = f32[2,8,128]{2,1,0:T(8,128)S(1)} collective-permute-done((f32[2,8,128]{2,1,0:T(8,128)S(1)}, f32[2,8,128]{2,1,0:T(8,128)S(1)}, u32[]{:S(2)}, u32[]{:S(2)}) %collective-permute-start.7) | collective-permute-done | bytes 8224 | tf_op jit(solution)/shard_map/ppermute | solution.py:133
  16.0 2.6 %collective-permute-start.9 = (f32[1,8,128]{2,1,0:T(8,128)S(1)}, f32[1,8,128]{2,1,0:T(8,128)S(1)}, u32[]{:S(2)}, u32[]{:S(2)}) collective-permute-start(f32[1,8,128]{2,1,0:T(8,128)S(1)} %slice.45), channel_id=1, source_target_pairs={{0,16},{4,20},{8,24},{12,28},{16,0},{20,4},{24,8},{28,12},{1,17},{... | collective-permute-start | bytes 12296 | tf_op jit(solution)/shard_map/ppermute | solution.py:133
  18.7 0.0 collective-permute-done.6
  18.7 0.1 collective-permute-start.8
  18.7 1.8 %collective-permute-done.9 = f32[1,8,128]{2,1,0:T(8,128)S(1)} collective-permute-done((f32[1,8,128]{2,1,0:T(8,128)S(1)}, f32[1,8,128]{2,1,0:T(8,128)S(1)}, u32[]{:S(2)}, u32[]{:S(2)}) %collective-permute-start.9) | collective-permute-done | bytes 4128 | tf_op jit(solution)/shard_map/ppermute | solution.py:133
  20.5 0.0 collective-permute-done.8
  20.5 0.6 %fusion.1 = f32[8,128]{1,0:T(8,128)} fusion(f32[1,8,128]{2,1,0:T(8,128)S(1)} %collective-permute-done.9, f32[2,8,128]{2,1,0:T(8,128)S(1)} %slice_add_fusion, f32[1,8,128]{2,1,0:T(8,128)S(1)} %collective-permute-done.8, f32[2,8,128]{2,1,0:T(8,128)S(1)} %add.25), kind=kLoop, calls=%fused_computation.4 | loop fusion | flops 3072 | bytes 20480 | tf_op jit(solution)/shard_map/add | solution.py:205
  (11 shorter events, 0.0 us)
Async XLA Ops:
  0.0 1.8 %collective-permute-start = (bf16[1,8,128]{2,1,0:T(8,128)(2,1)}, bf16[1,8,128]{2,1,0:T(8,128)(2,1)S(1)}, u32[]{:S(2)}, u32[]{:S(2)}) collective-permute-start(bf16[1,8,128]{2,1,0:T(8,128)(2,1)} %bitcast.10), channel_id=1, source_target_pairs={{0,1},{1,0},{2,3},{3,2},{4,5},{5,4},{6,7},{7,6},{8,9},{9,8},{10,11... | collective-permute-start | bytes 6152 | tf_op jit(solution)/shard_map/ppermute | solution.py:133
  1.8 4.5 %collective-permute-start.1 = (bf16[2,8,128]{2,1,0:T(8,128)(2,1)S(1)}, bf16[2,8,128]{2,1,0:T(8,128)(2,1)S(1)}, u32[]{:S(2)}, u32[]{:S(2)}) collective-permute-start(bf16[2,8,128]{2,1,0:T(8,128)(2,1)S(1)} %pad_maximum_fusion.1.pair_ref.refs_0_), channel_id=1, source_target_pairs={{0,9},{1,8},{2,11},{3,10},{4,13},{5,12},{6,15},{7,14},{8,1},{9,0},... | collective-permute-start | bytes 12296 | tf_op jit(solution)/shard_map/ppermute | solution.py:137
  4.5 3.5 %collective-permute-start.3 = (bf16[2,8,128]{2,1,0:T(8,128)(2,1)S(1)}, bf16[2,8,128]{2,1,0:T(8,128)(2,1)S(1)}, u32[]{:S(2)}, u32[]{:S(2)}) collective-permute-start(bf16[2,8,128]{2,1,0:T(8,128)(2,1)S(1)} %pad_maximum_fusion.1.pair_ref.refs_0_), channel_id=1, source_target_pairs={{0,3},{1,2},{2,1},{3,0},{4,7},{5,6},{6,5},{7,4},{8,11},{9,10},{10,... | collective-permute-start | bytes 12296 | tf_op jit(solution)/shard_map/ppermute | solution.py:133
  6.3 3.5 %collective-permute-start.2 = (bf16[4,8,128]{2,1,0:T(8,128)(2,1)S(1)}, bf16[4,8,128]{2,1,0:T(8,128)(2,1)S(1)}, u32[]{:S(2)}, u32[]{:S(2)}) collective-permute-start(bf16[4,8,128]{2,1,0:T(8,128)(2,1)S(1)} %shard_map.56), channel_id=1, source_target_pairs={{0,5},{1,4},{2,7},{3,6},{4,1},{5,0},{6,3},{7,2},{8,13},{9,12},{10,... | collective-permute-start | bytes 24584 | tf_op jit(solution)/shard_map/ppermute | solution.py:137
  8.5 3.8 %collective-permute-start.5 = (f32[4,8,128]{2,1,0:T(8,128)S(1)}, f32[4,8,128]{2,1,0:T(8,128)S(1)}, u32[]{:S(2)}, u32[]{:S(2)}) collective-permute-start(f32[4,8,128]{2,1,0:T(8,128)S(1)} %get-tuple-element.31), channel_id=1, source_target_pairs={{0,8},{4,12},{8,0},{12,4},{16,24},{20,28},{24,16},{28,20},{1,9},{5... | collective-permute-start | bytes 49160 | tf_op jit(solution)/shard_map/ppermute | solution.py:133
  9.9 4.0 %collective-permute-start.4 = (bf16[4,8,128]{2,1,0:T(8,128)(2,1)S(1)}, bf16[4,8,128]{2,1,0:T(8,128)(2,1)S(1)}, u32[]{:S(2)}, u32[]{:S(2)}) collective-permute-start(bf16[4,8,128]{2,1,0:T(8,128)(2,1)S(1)} %pad_maximum_fusion), channel_id=1, source_target_pairs={{0,17},{1,16},{2,19},{3,18},{4,21},{5,20},{6,23},{7,22},{8,25},{9,... | collective-permute-start | bytes 24584 | tf_op jit(solution)/shard_map/ppermute | solution.py:137
  12.3 3.7 %collective-permute-start.7 = (f32[2,8,128]{2,1,0:T(8,128)S(1)}, f32[2,8,128]{2,1,0:T(8,128)S(1)}, u32[]{:S(2)}, u32[]{:S(2)}) collective-permute-start(f32[2,8,128]{2,1,0:T(8,128)S(1)} %slice.44), channel_id=1, source_target_pairs={{0,4},{4,0},{8,12},{12,8},{16,20},{20,16},{24,28},{28,24},{1,5},{5... | collective-permute-start | bytes 24584 | tf_op jit(solution)/shard_map/ppermute | solution.py:133
  14.5 4.2 %collective-permute-start.6 = (f32[2,8,128]{2,1,0:T(8,128)S(1)}, f32[2,8,128]{2,1,0:T(8,128)S(1)}, u32[]{:S(2)}, u32[]{:S(2)}) collective-permute-start(f32[2,8,128]{2,1,0:T(8,128)S(1)} %get-tuple-element.37), channel_id=1, source_target_pairs={{0,3},{1,2},{2,1},{3,0},{4,7},{5,6},{6,5},{7,4},{8,11},{9,10},{10,... | collective-permute-start | bytes 24584 | tf_op jit(solution)/shard_map/ppermute | solution.py:133
  16.0 4.5 %collective-permute-start.9 = (f32[1,8,128]{2,1,0:T(8,128)S(1)}, f32[1,8,128]{2,1,0:T(8,128)S(1)}, u32[]{:S(2)}, u32[]{:S(2)}) collective-permute-start(f32[1,8,128]{2,1,0:T(8,128)S(1)} %slice.45), channel_id=1, source_target_pairs={{0,16},{4,20},{8,24},{12,28},{16,0},{20,4},{24,8},{28,12},{1,17},{... | collective-permute-start | bytes 12296 | tf_op jit(solution)/shard_map/ppermute | solution.py:133
  18.7 1.9 %collective-permute-start.8 = (f32[1,8,128]{2,1,0:T(8,128)S(1)}, f32[1,8,128]{2,1,0:T(8,128)S(1)}, u32[]{:S(2)}, u32[]{:S(2)}) collective-permute-start(f32[1,8,128]{2,1,0:T(8,128)S(1)} %slice.47), channel_id=1, source_target_pairs={{0,1},{1,0},{2,3},{3,2},{4,5},{5,4},{6,7},{7,6},{8,9},{9,8},{10,11... | collective-permute-start | bytes 12296 | tf_op jit(solution)/shard_map/ppermute | solution.py:133

commit v2 on v1

--- a/solution.py
+++ b/solution.py
@@ -72,7 +72,7 @@
     while bit < cols_axis:
         crossed = crossed ^ ((far_rows & bit) // bit)
         bit *= 2
-    spread = (far_cols & 2) * (rows_axis // 4) + (far_cols & 1) * (rows_axis // 4) + (far_cols >> 2)
+    spread = (far_cols & 1) * (rows_axis // 2) + (far_cols & 2) * (rows_axis // 8) + (far_cols >> 2)
     one_hots(crossed, spread, col_choice, col_sums)
     order = (far_cols & 1) * 2 + (far_cols & 2) // 2 + (far_cols >> 2) * 4
     one_hots(order, crossed, row_choice, row_sums)
@@ -175,7 +175,7 @@
     row_new = crossing(row_sent, 1)
     col_stack[-1] = after(col_stack[-1], row_sent)
     col_keep, col_send = terms(0, rows_axis, col_choice, col_sums, col_stack)
-    col_in = swapped(col_send, "row", 2)
+    col_in = swapped(col_send, "row", 1)
     step = 2
     while 2 * step < rows_axis:
         row_new = after(row_new, col_send)
@@ -186,7 +186,7 @@
         row_new = crossing(row_sent, step)
     col_terms = col_keep + after(col_in, row_sent)
     down = rows_axis // 4
-    col_in = swapped(col_terms[down:], "row", 1)
+    col_in = swapped(col_terms[down:], "row", 2)
     mine.append(after(row_new, col_terms))
     row_keep, row_send = terms(1, cols_axis, row_choice, row_sums, mine)
     across = cols_axis // 2

time: 21.3 us -> 21.3 us (level)
  starting transfers between devices: 15.1 us -> 14.8 us
  waiting for transfers between devices: 2.3 us -> 2.56 us
    ppermute x7, starting transfers between devices: 8.27 us -> 7.84 us  [swapped(): lax.ppermute(x, axis, [(d, d ^ step) for d in range(lax.axis_size(axis))])]
    ppermute x7, waiting for transfers between devices: 2.21 us -> 2.46 us  [swapped(): lax.ppermute(x, axis, [(d, d ^ step) for d in range(lax.axis_size(axis))])]
where the time goes in v2:
time: 21.3 us; the launch traced here: 21.1 us
  starting transfers between devices  14.8 us (69%)
  waiting for transfers between devices  2.56 us (12%)
  Pallas kernels  2.39 us (11%)
  between operations  0.72 us (3%)
  other arithmetic  0.62 us (3%)
    ppermute x7, starting transfers between devices, swapped(): lax.ppermute(x, axis, [(d, d ^ step) for d in range(lax.axis_size(axis))])  7.84 us
    ppermute x3, starting transfers between devices, crossing(): return lax.ppermute(x, ('row', 'col'), pairs)  6.98 us
    ppermute x7, waiting for transfers between devices, swapped(): lax.ppermute(x, axis, [(d, d ^ step) for d in range(lax.axis_size(axis))])  2.46 us
    pallas_call x1, Pallas kernels, per_device(): small_kernel(made_ready, [one_hot(slots, cols_axis), one_hot(rows_axis, s...  1.29 us
    pallas_call x2, Pallas kernels, terms(): small_kernel(functools.partial(slot_sums, contract), [half, half], [SCALA...  1.1 us
    add x1, other arithmetic, per_device(): row_terms[0] + row_in[0] + (col_terms[0] + after(col_in, row_terms)[0])  0.6 us
  transfers between devices with their start and end apart: 10, of which 4 were waited for; matrix products, arithmetic and copies ran while one was open for 0% of the time, Pallas kernels for 11%

profile of v2, /device:TPU:0, one launch (start us, length us, event | category | flops | bytes accessed | tf_op | source)
XLA Modules:
  0.0 21.1 jit_solution(4393211682372246845)
XLA Ops:
  0.0 0.5 %collective-permute-start = (bf16[1,8,128]{2,1,0:T(8,128)(2,1)}, bf16[1,8,128]{2,1,0:T(8,128)(2,1)S(1)}, u32[]{:S(2)}, u32[]{:S(2)}) collective-permute-start(bf16[1,8,128]{2,1,0:T(8,128)(2,1)} %bitcast.10), channel_id=1, source_target_pairs={{0,1},{1,0},{2,3},{3,2},{4,5},{5,4},{6,7},{7,6},{8,9},{9,8},{10,11... | collective-permute-start | bytes 6152 | tf_op jit(solution)/shard_map/ppermute | solution.py:133
  0.5 1.3 %shard_map.55 = (bf16[256,32]{1,0:T(8,128)(2,1)S(1)}, bf16[64,256]{1,0:T(8,128)(2,1)S(1)}, bf16[256,64]{1,0:T(8,128)(2,1)S(1)}, bf16[32,256]{1,0:T(8,128)(2,1)S(...) custom-call(s32[1,32]{1,0:T(1,128)} %bitcast.11, s32[1,32]{1,0:T(1,128)} %bitcast.12, ...), custom_call_target="tpu_custom_call" | custom-call | tf_op jit(solution)/shard_map/pallas_call | solution.py:155
  1.8 0.0 collective-permute-done
  1.8 2.8 %collective-permute-start.1 = (bf16[2,8,128]{2,1,0:T(8,128)(2,1)S(1)}, bf16[2,8,128]{2,1,0:T(8,128)(2,1)S(1)}, u32[]{:S(2)}, u32[]{:S(2)}) collective-permute-start(bf16[2,8,128]{2,1,0:T(8,128)(2,1)S(1)} %pad_maximum_fusion.1.pair_ref.refs_0_), channel_id=1, source_target_pairs={{0,9},{1,8},{2,11},{3,10},{4,13},{5,12},{6,15},{7,14},{8,1},{9,0},... | collective-permute-start | bytes 12296 | tf_op jit(solution)/shard_map/ppermute | solution.py:137
  4.5 1.1 %collective-permute-start.3 = (bf16[2,8,128]{2,1,0:T(8,128)(2,1)S(1)}, bf16[2,8,128]{2,1,0:T(8,128)(2,1)S(1)}, u32[]{:S(2)}, u32[]{:S(2)}) collective-permute-start(bf16[2,8,128]{2,1,0:T(8,128)(2,1)S(1)} %pad_maximum_fusion.1.pair_ref.refs_0_), channel_id=1, source_target_pairs={{0,3},{1,2},{2,1},{3,0},{4,7},{5,6},{6,5},{7,4},{8,11},{9,10},{10,... | collective-permute-start | bytes 12296 | tf_op jit(solution)/shard_map/ppermute | solution.py:133
  6.3 0.0 collective-permute-done.1.new_ref
  6.3 1.7 %collective-permute-start.2 = (bf16[4,8,128]{2,1,0:T(8,128)(2,1)S(1)}, bf16[4,8,128]{2,1,0:T(8,128)(2,1)S(1)}, u32[]{:S(2)}, u32[]{:S(2)}) collective-permute-start(bf16[4,8,128]{2,1,0:T(8,128)(2,1)S(1)} %shard_map.56), channel_id=1, source_target_pairs={{0,5},{1,4},{2,7},{3,6},{4,1},{5,0},{6,3},{7,2},{8,13},{9,12},{10,... | collective-permute-start | bytes 24584 | tf_op jit(solution)/shard_map/ppermute | solution.py:137
  8.0 0.0 collective-permute-done.3.refs_1_
  8.0 0.5 %shard_map.57 = (f32[4,8,128]{2,1,0:T(8,128)S(1)}, f32[4,8,128]{2,1,0:T(8,128)S(1)}) custom-call(s32[1,1]{1,0:T(1,128)S(6)} %copy.6.filled_ref, bf16[256,32]{1,0:T(8,128)(2,1)S(1)} %get-tuple-element.28.choice_ref, bf16[64,256]{1,0:T(8,128)(2,1)S(1)} %get-tuple-element.29.sums_ref, bf16[32,128,128]{2,1,0:T(8,128)(2,1)S(1)} %get-tuple-element.27.tiles_ref, ...), custom_call_target="tpu_custom_call" | custom-call | tf_op jit(solution)/shard_map/pallas_call | solution.py:150
  8.5 1.1 %collective-permute-start.5 = (f32[4,8,128]{2,1,0:T(8,128)S(1)}, f32[4,8,128]{2,1,0:T(8,128)S(1)}, u32[]{:S(2)}, u32[]{:S(2)}) collective-permute-start(f32[4,8,128]{2,1,0:T(8,128)S(1)} %get-tuple-element.31), channel_id=1, source_target_pairs={{0,4},{4,0},{8,12},{12,8},{16,20},{20,16},{24,28},{28,24},{1,5},{5... | collective-permute-start | bytes 49160 | tf_op jit(solution)/shard_map/ppermute | solution.py:133
  9.7 0.0 collective-permute-done.2
  9.7 2.5 %collective-permute-start.4 = (bf16[4,8,128]{2,1,0:T(8,128)(2,1)S(1)}, bf16[4,8,128]{2,1,0:T(8,128)(2,1)S(1)}, u32[]{:S(2)}, u32[]{:S(2)}) collective-permute-start(bf16[4,8,128]{2,1,0:T(8,128)(2,1)S(1)} %pad_maximum_fusion), channel_id=1, source_target_pairs={{0,17},{1,16},{2,19},{3,18},{4,21},{5,20},{6,23},{7,22},{8,25},{9,... | collective-permute-start | bytes 24584 | tf_op jit(solution)/shard_map/ppermute | solution.py:137
  12.2 0.1 collective-permute-done.5
  12.3 1.3 %collective-permute-start.7 = (f32[2,8,128]{2,1,0:T(8,128)S(1)}, f32[2,8,128]{2,1,0:T(8,128)S(1)}, u32[]{:S(2)}, u32[]{:S(2)}) collective-permute-start(f32[2,8,128]{2,1,0:T(8,128)S(1)} %slice.44), channel_id=1, source_target_pairs={{0,8},{4,12},{8,0},{12,4},{16,24},{20,28},{24,16},{28,20},{1,9},{5... | collective-permute-start | bytes 24584 | tf_op jit(solution)/shard_map/ppermute | solution.py:133
  13.6 0.1 collective-permute-done.4.refs_3_
  13.7 0.6 %shard_map.58 = (f32[2,8,128]{2,1,0:T(8,128)S(1)}, f32[2,8,128]{2,1,0:T(8,128)S(1)}) custom-call(s32[1,1]{1,0:T(1,128)S(6)} %copy.6.filled_ref, bf16[256,64]{1,0:T(8,128)(2,1)S(1)} %get-tuple-element.25.choice_ref, bf16[32,256]{1,0:T(8,128)(2,1)S(1)} %get-tuple-element.26.sums_ref, bf16[32,128,128]{2,1,0:T(8,128)(2,1)S(1)} %get-tuple-element.27.tiles_ref, ...), custom_call_target="tpu_custom_call" | custom-call | tf_op jit(solution)/shard_map/pallas_call | solution.py:150
  14.3 1.2 %collective-permute-start.6 = (f32[2,8,128]{2,1,0:T(8,128)S(1)}, f32[2,8,128]{2,1,0:T(8,128)S(1)}, u32[]{:S(2)}, u32[]{:S(2)}) collective-permute-start(f32[2,8,128]{2,1,0:T(8,128)S(1)} %get-tuple-element.37), channel_id=1, source_target_pairs={{0,3},{1,2},{2,1},{3,0},{4,7},{5,6},{6,5},{7,4},{8,11},{9,10},{10,... | collective-permute-start | bytes 24584 | tf_op jit(solution)/shard_map/ppermute | solution.py:133
  15.5 0.5 %collective-permute-done.7 = f32[2,8,128]{2,1,0:T(8,128)S(1)} collective-permute-done((f32[2,8,128]{2,1,0:T(8,128)S(1)}, f32[2,8,128]{2,1,0:T(8,128)S(1)}, u32[]{:S(2)}, u32[]{:S(2)}) %collective-permute-start.7) | collective-permute-done | bytes 8224 | tf_op jit(solution)/shard_map/ppermute | solution.py:133
  16.0 2.6 %collective-permute-start.9 = (f32[1,8,128]{2,1,0:T(8,128)S(1)}, f32[1,8,128]{2,1,0:T(8,128)S(1)}, u32[]{:S(2)}, u32[]{:S(2)}) collective-permute-start(f32[1,8,128]{2,1,0:T(8,128)S(1)} %slice.45), channel_id=1, source_target_pairs={{0,16},{4,20},{8,24},{12,28},{16,0},{20,4},{24,8},{28,12},{1,17},{... | collective-permute-start | bytes 12296 | tf_op jit(solution)/shard_map/ppermute | solution.py:133
  18.6 0.0 collective-permute-done.6
  18.6 0.1 collective-permute-start.8
  18.7 1.9 %collective-permute-done.9 = f32[1,8,128]{2,1,0:T(8,128)S(1)} collective-permute-done((f32[1,8,128]{2,1,0:T(8,128)S(1)}, f32[1,8,128]{2,1,0:T(8,128)S(1)}, u32[]{:S(2)}, u32[]{:S(2)}) %collective-permute-start.9) | collective-permute-done | bytes 4128 | tf_op jit(solution)/shard_map/ppermute | solution.py:133
  20.5 0.0 collective-permute-done.8
  20.5 0.6 %fusion.1 = f32[8,128]{1,0:T(8,128)} fusion(f32[1,8,128]{2,1,0:T(8,128)S(1)} %collective-permute-done.9, f32[2,8,128]{2,1,0:T(8,128)S(1)} %slice_add_fusion, f32[1,8,128]{2,1,0:T(8,128)S(1)} %collective-permute-done.8, f32[2,8,128]{2,1,0:T(8,128)S(1)} %add.25), kind=kLoop, calls=%fused_computation.4 | loop fusion | flops 3072 | bytes 20480 | tf_op jit(solution)/shard_map/add | solution.py:205
  (11 shorter events, 0.0 us)
Async XLA Ops:
  0.0 1.8 %collective-permute-start = (bf16[1,8,128]{2,1,0:T(8,128)(2,1)}, bf16[1,8,128]{2,1,0:T(8,128)(2,1)S(1)}, u32[]{:S(2)}, u32[]{:S(2)}) collective-permute-start(bf16[1,8,128]{2,1,0:T(8,128)(2,1)} %bitcast.10), channel_id=1, source_target_pairs={{0,1},{1,0},{2,3},{3,2},{4,5},{5,4},{6,7},{7,6},{8,9},{9,8},{10,11... | collective-permute-start | bytes 6152 | tf_op jit(solution)/shard_map/ppermute | solution.py:133
  1.8 4.5 %collective-permute-start.1 = (bf16[2,8,128]{2,1,0:T(8,128)(2,1)S(1)}, bf16[2,8,128]{2,1,0:T(8,128)(2,1)S(1)}, u32[]{:S(2)}, u32[]{:S(2)}) collective-permute-start(bf16[2,8,128]{2,1,0:T(8,128)(2,1)S(1)} %pad_maximum_fusion.1.pair_ref.refs_0_), channel_id=1, source_target_pairs={{0,9},{1,8},{2,11},{3,10},{4,13},{5,12},{6,15},{7,14},{8,1},{9,0},... | collective-permute-start | bytes 12296 | tf_op jit(solution)/shard_map/ppermute | solution.py:137
  4.5 3.5 %collective-permute-start.3 = (bf16[2,8,128]{2,1,0:T(8,128)(2,1)S(1)}, bf16[2,8,128]{2,1,0:T(8,128)(2,1)S(1)}, u32[]{:S(2)}, u32[]{:S(2)}) collective-permute-start(bf16[2,8,128]{2,1,0:T(8,128)(2,1)S(1)} %pad_maximum_fusion.1.pair_ref.refs_0_), channel_id=1, source_target_pairs={{0,3},{1,2},{2,1},{3,0},{4,7},{5,6},{6,5},{7,4},{8,11},{9,10},{10,... | collective-permute-start | bytes 12296 | tf_op jit(solution)/shard_map/ppermute | solution.py:133
  6.3 3.4 %collective-permute-start.2 = (bf16[4,8,128]{2,1,0:T(8,128)(2,1)S(1)}, bf16[4,8,128]{2,1,0:T(8,128)(2,1)S(1)}, u32[]{:S(2)}, u32[]{:S(2)}) collective-permute-start(bf16[4,8,128]{2,1,0:T(8,128)(2,1)S(1)} %shard_map.56), channel_id=1, source_target_pairs={{0,5},{1,4},{2,7},{3,6},{4,1},{5,0},{6,3},{7,2},{8,13},{9,12},{10,... | collective-permute-start | bytes 24584 | tf_op jit(solution)/shard_map/ppermute | solution.py:137
  8.5 3.8 %collective-permute-start.5 = (f32[4,8,128]{2,1,0:T(8,128)S(1)}, f32[4,8,128]{2,1,0:T(8,128)S(1)}, u32[]{:S(2)}, u32[]{:S(2)}) collective-permute-start(f32[4,8,128]{2,1,0:T(8,128)S(1)} %get-tuple-element.31), channel_id=1, source_target_pairs={{0,4},{4,0},{8,12},{12,8},{16,20},{20,16},{24,28},{28,24},{1,5},{5... | collective-permute-start | bytes 49160 | tf_op jit(solution)/shard_map/ppermute | solution.py:133
  9.7 4.0 %collective-permute-start.4 = (bf16[4,8,128]{2,1,0:T(8,128)(2,1)S(1)}, bf16[4,8,128]{2,1,0:T(8,128)(2,1)S(1)}, u32[]{:S(2)}, u32[]{:S(2)}) collective-permute-start(bf16[4,8,128]{2,1,0:T(8,128)(2,1)S(1)} %pad_maximum_fusion), channel_id=1, source_target_pairs={{0,17},{1,16},{2,19},{3,18},{4,21},{5,20},{6,23},{7,22},{8,25},{9,... | collective-permute-start | bytes 24584 | tf_op jit(solution)/shard_map/ppermute | solution.py:137
  12.3 3.7 %collective-permute-start.7 = (f32[2,8,128]{2,1,0:T(8,128)S(1)}, f32[2,8,128]{2,1,0:T(8,128)S(1)}, u32[]{:S(2)}, u32[]{:S(2)}) collective-permute-start(f32[2,8,128]{2,1,0:T(8,128)S(1)} %slice.44), channel_id=1, source_target_pairs={{0,8},{4,12},{8,0},{12,4},{16,24},{20,28},{24,16},{28,20},{1,9},{5... | collective-permute-start | bytes 24584 | tf_op jit(solution)/shard_map/ppermute | solution.py:133
  14.3 4.3 %collective-permute-start.6 = (f32[2,8,128]{2,1,0:T(8,128)S(1)}, f32[2,8,128]{2,1,0:T(8,128)S(1)}, u32[]{:S(2)}, u32[]{:S(2)}) collective-permute-start(f32[2,8,128]{2,1,0:T(8,128)S(1)} %get-tuple-element.37), channel_id=1, source_target_pairs={{0,3},{1,2},{2,1},{3,0},{4,7},{5,6},{6,5},{7,4},{8,11},{9,10},{10,... | collective-permute-start | bytes 24584 | tf_op jit(solution)/shard_map/ppermute | solution.py:133
  16.0 4.5 %collective-permute-start.9 = (f32[1,8,128]{2,1,0:T(8,128)S(1)}, f32[1,8,128]{2,1,0:T(8,128)S(1)}, u32[]{:S(2)}, u32[]{:S(2)}) collective-permute-start(f32[1,8,128]{2,1,0:T(8,128)S(1)} %slice.45), channel_id=1, source_target_pairs={{0,16},{4,20},{8,24},{12,28},{16,0},{20,4},{24,8},{28,12},{1,17},{... | collective-permute-start | bytes 12296 | tf_op jit(solution)/shard_map/ppermute | solution.py:133
  18.6 1.9 %collective-permute-start.8 = (f32[1,8,128]{2,1,0:T(8,128)S(1)}, f32[1,8,128]{2,1,0:T(8,128)S(1)}, u32[]{:S(2)}, u32[]{:S(2)}) collective-permute-start(f32[1,8,128]{2,1,0:T(8,128)S(1)} %slice.47), channel_id=1, source_target_pairs={{0,1},{1,0},{2,3},{3,2},{4,5},{5,4},{6,7},{7,6},{8,9},{9,8},{10,11... | collective-permute-start | bytes 12296 | tf_op jit(solution)/shard_map/ppermute | solution.py:133

commit v3 on v0

--- a/solution.py
+++ b/solution.py
@@ -60,9 +60,10 @@
         pltpu.make_async_copy(tiles_ref.at[pl.ds(k * half, half)], stored_ref.at[pl.ds(k * half, half)], arrived.at[3 + k])
         for k in range(2)
     ]
-    for load in loads[:4]:
+    loads[3].start()
+    loads[4].start(priority=1)
+    for load in loads[:3]:
         load.start()
-    loads[4].start(priority=1)
     for load in loads[:2]:
         load.wait()
     rows_axis, cols_axis = lax.axis_size("row"), lax.axis_size("col")

time: 21.3 us -> 21.3 us (level)
  no operation moved by 1% of the time
where the time goes in v3:
time: 21.3 us; the launch traced here: 21.1 us
  starting transfers between devices  14.8 us (69%)
  waiting for transfers between devices  2.55 us (12%)
  Pallas kernels  2.39 us (11%)
  between operations  0.72 us (3%)
  other arithmetic  0.62 us (3%)
    ppermute x7, starting transfers between devices, swapped(): lax.ppermute(x, axis, [(d, d ^ step) for d in range(lax.axis_size(axis))])  7.89 us
    ppermute x3, starting transfers between devices, crossing(): return lax.ppermute(x, ('row', 'col'), pairs)  6.93 us
    ppermute x7, waiting for transfers between devices, swapped(): lax.ppermute(x, axis, [(d, d ^ step) for d in range(lax.axis_size(axis))])  2.49 us
    pallas_call x1, Pallas kernels, per_device(): small_kernel(made_ready, [one_hot(slots, cols_axis), one_hot(rows_axis, s...  1.29 us
    pallas_call x2, Pallas kernels, terms(): small_kernel(functools.partial(slot_sums, contract), [half, half], [SCALA...  1.1 us
    add x1, other arithmetic, per_device(): row_terms[0] + row_in[0] + (col_terms[0] + after(col_in, row_terms)[0])  0.6 us
  transfers between devices with their start and end apart: 10, of which 4 were waited for; matrix products, arithmetic and copies ran while one was open for 0% of the time, Pallas kernels for 11%

profile of v3, /device:TPU:0, one launch (start us, length us, event | category | flops | bytes accessed | tf_op | source)
XLA Modules:
  0.0 21.1 jit_solution(13543769111957951064)
XLA Ops:
  0.0 0.5 %collective-permute-start = (bf16[1,8,128]{2,1,0:T(8,128)(2,1)}, bf16[1,8,128]{2,1,0:T(8,128)(2,1)S(1)}, u32[]{:S(2)}, u32[]{:S(2)}) collective-permute-start(bf16[1,8,128]{2,1,0:T(8,128)(2,1)} %bitcast.10), channel_id=1, source_target_pairs={{0,1},{1,0},{2,3},{3,2},{4,5},{5,4},{6,7},{7,6},{8,9},{9,8},{10,11... | collective-permute-start | bytes 6152 | tf_op jit(solution)/shard_map/ppermute | solution.py:133
  0.5 1.3 %shard_map.55 = (bf16[256,32]{1,0:T(8,128)(2,1)S(1)}, bf16[64,256]{1,0:T(8,128)(2,1)S(1)}, bf16[256,64]{1,0:T(8,128)(2,1)S(1)}, bf16[32,256]{1,0:T(8,128)(2,1)S(...) custom-call(s32[1,32]{1,0:T(1,128)} %bitcast.11, s32[1,32]{1,0:T(1,128)} %bitcast.12, ...), custom_call_target="tpu_custom_call" | custom-call | tf_op jit(solution)/shard_map/pallas_call | solution.py:155
  1.8 0.0 collective-permute-done
  1.8 2.7 %collective-permute-start.1 = (bf16[2,8,128]{2,1,0:T(8,128)(2,1)S(1)}, bf16[2,8,128]{2,1,0:T(8,128)(2,1)S(1)}, u32[]{:S(2)}, u32[]{:S(2)}) collective-permute-start(bf16[2,8,128]{2,1,0:T(8,128)(2,1)S(1)} %pad_maximum_fusion.1.pair_ref.refs_0_), channel_id=1, source_target_pairs={{0,5},{1,4},{2,7},{3,6},{4,1},{5,0},{6,3},{7,2},{8,13},{9,12},{10,... | collective-permute-start | bytes 12296 | tf_op jit(solution)/shard_map/ppermute | solution.py:137
  4.5 1.1 %collective-permute-start.3 = (bf16[2,8,128]{2,1,0:T(8,128)(2,1)S(1)}, bf16[2,8,128]{2,1,0:T(8,128)(2,1)S(1)}, u32[]{:S(2)}, u32[]{:S(2)}) collective-permute-start(bf16[2,8,128]{2,1,0:T(8,128)(2,1)S(1)} %pad_maximum_fusion.1.pair_ref.refs_0_), channel_id=1, source_target_pairs={{0,3},{1,2},{2,1},{3,0},{4,7},{5,6},{6,5},{7,4},{8,11},{9,10},{10,... | collective-permute-start | bytes 12296 | tf_op jit(solution)/shard_map/ppermute | solution.py:133
  6.2 0.0 collective-permute-done.1.new_ref
  6.2 1.8 %collective-permute-start.2 = (bf16[4,8,128]{2,1,0:T(8,128)(2,1)S(1)}, bf16[4,8,128]{2,1,0:T(8,128)(2,1)S(1)}, u32[]{:S(2)}, u32[]{:S(2)}) collective-permute-start(bf16[4,8,128]{2,1,0:T(8,128)(2,1)S(1)} %shard_map.56), channel_id=1, source_target_pairs={{0,9},{1,8},{2,11},{3,10},{4,13},{5,12},{6,15},{7,14},{8,1},{9,0},... | collective-permute-start | bytes 24584 | tf_op jit(solution)/shard_map/ppermute | solution.py:137
  8.0 0.0 collective-permute-done.3.refs_1_
  8.0 0.5 %shard_map.57 = (f32[4,8,128]{2,1,0:T(8,128)S(1)}, f32[4,8,128]{2,1,0:T(8,128)S(1)}) custom-call(s32[1,1]{1,0:T(1,128)S(6)} %copy.6.filled_ref, bf16[256,32]{1,0:T(8,128)(2,1)S(1)} %get-tuple-element.28.choice_ref, bf16[64,256]{1,0:T(8,128)(2,1)S(1)} %get-tuple-element.29.sums_ref, bf16[32,128,128]{2,1,0:T(8,128)(2,1)S(1)} %get-tuple-element.27.tiles_ref, ...), custom_call_target="tpu_custom_call" | custom-call | tf_op jit(solution)/shard_map/pallas_call | solution.py:150
  8.5 1.1 %collective-permute-start.5 = (f32[4,8,128]{2,1,0:T(8,128)S(1)}, f32[4,8,128]{2,1,0:T(8,128)S(1)}, u32[]{:S(2)}, u32[]{:S(2)}) collective-permute-start(f32[4,8,128]{2,1,0:T(8,128)S(1)} %get-tuple-element.31), channel_id=1, source_target_pairs={{0,8},{4,12},{8,0},{12,4},{16,24},{20,28},{24,16},{28,20},{1,9},{5... | collective-permute-start | bytes 49160 | tf_op jit(solution)/shard_map/ppermute | solution.py:133
  9.7 0.0 collective-permute-done.2
  9.7 2.5 %collective-permute-start.4 = (bf16[4,8,128]{2,1,0:T(8,128)(2,1)S(1)}, bf16[4,8,128]{2,1,0:T(8,128)(2,1)S(1)}, u32[]{:S(2)}, u32[]{:S(2)}) collective-permute-start(bf16[4,8,128]{2,1,0:T(8,128)(2,1)S(1)} %pad_maximum_fusion), channel_id=1, source_target_pairs={{0,17},{1,16},{2,19},{3,18},{4,21},{5,20},{6,23},{7,22},{8,25},{9,... | collective-permute-start | bytes 24584 | tf_op jit(solution)/shard_map/ppermute | solution.py:137
  12.2 0.2 collective-permute-done.5
  12.3 1.3 %collective-permute-start.7 = (f32[2,8,128]{2,1,0:T(8,128)S(1)}, f32[2,8,128]{2,1,0:T(8,128)S(1)}, u32[]{:S(2)}, u32[]{:S(2)}) collective-permute-start(f32[2,8,128]{2,1,0:T(8,128)S(1)} %slice.44), channel_id=1, source_target_pairs={{0,4},{4,0},{8,12},{12,8},{16,20},{20,16},{24,28},{28,24},{1,5},{5... | collective-permute-start | bytes 24584 | tf_op jit(solution)/shard_map/ppermute | solution.py:133
  13.7 0.1 collective-permute-done.4.refs_3_
  13.7 0.6 %shard_map.58 = (f32[2,8,128]{2,1,0:T(8,128)S(1)}, f32[2,8,128]{2,1,0:T(8,128)S(1)}) custom-call(s32[1,1]{1,0:T(1,128)S(6)} %copy.6.filled_ref, bf16[256,64]{1,0:T(8,128)(2,1)S(1)} %get-tuple-element.25.choice_ref, bf16[32,256]{1,0:T(8,128)(2,1)S(1)} %get-tuple-element.26.sums_ref, bf16[32,128,128]{2,1,0:T(8,128)(2,1)S(1)} %get-tuple-element.27.tiles_ref, ...), custom_call_target="tpu_custom_call" | custom-call | tf_op jit(solution)/shard_map/pallas_call | solution.py:150
  14.3 1.2 %collective-permute-start.6 = (f32[2,8,128]{2,1,0:T(8,128)S(1)}, f32[2,8,128]{2,1,0:T(8,128)S(1)}, u32[]{:S(2)}, u32[]{:S(2)}) collective-permute-start(f32[2,8,128]{2,1,0:T(8,128)S(1)} %get-tuple-element.37), channel_id=1, source_target_pairs={{0,3},{1,2},{2,1},{3,0},{4,7},{5,6},{6,5},{7,4},{8,11},{9,10},{10,... | collective-permute-start | bytes 24584 | tf_op jit(solution)/shard_map/ppermute | solution.py:133
  15.5 0.5 %collective-permute-done.7 = f32[2,8,128]{2,1,0:T(8,128)S(1)} collective-permute-done((f32[2,8,128]{2,1,0:T(8,128)S(1)}, f32[2,8,128]{2,1,0:T(8,128)S(1)}, u32[]{:S(2)}, u32[]{:S(2)}) %collective-permute-start.7) | collective-permute-done | bytes 8224 | tf_op jit(solution)/shard_map/ppermute | solution.py:133
  16.0 2.6 %collective-permute-start.9 = (f32[1,8,128]{2,1,0:T(8,128)S(1)}, f32[1,8,128]{2,1,0:T(8,128)S(1)}, u32[]{:S(2)}, u32[]{:S(2)}) collective-permute-start(f32[1,8,128]{2,1,0:T(8,128)S(1)} %slice.45), channel_id=1, source_target_pairs={{0,16},{4,20},{8,24},{12,28},{16,0},{20,4},{24,8},{28,12},{1,17},{... | collective-permute-start | bytes 12296 | tf_op jit(solution)/shard_map/ppermute | solution.py:133
  18.6 0.0 collective-permute-done.6
  18.6 0.1 collective-permute-start.8
  18.7 1.8 %collective-permute-done.9 = f32[1,8,128]{2,1,0:T(8,128)S(1)} collective-permute-done((f32[1,8,128]{2,1,0:T(8,128)S(1)}, f32[1,8,128]{2,1,0:T(8,128)S(1)}, u32[]{:S(2)}, u32[]{:S(2)}) %collective-permute-start.9) | collective-permute-done | bytes 4128 | tf_op jit(solution)/shard_map/ppermute | solution.py:133
  20.5 0.0 collective-permute-done.8
  20.5 0.6 %fusion.1 = f32[8,128]{1,0:T(8,128)} fusion(f32[1,8,128]{2,1,0:T(8,128)S(1)} %collective-permute-done.9, f32[2,8,128]{2,1,0:T(8,128)S(1)} %slice_add_fusion, f32[1,8,128]{2,1,0:T(8,128)S(1)} %collective-permute-done.8, f32[2,8,128]{2,1,0:T(8,128)S(1)} %add.25), kind=kLoop, calls=%fused_computation.4 | loop fusion | flops 3072 | bytes 20480 | tf_op jit(solution)/shard_map/add | solution.py:205
  (11 shorter events, 0.0 us)
Async XLA Ops:
  0.0 1.8 %collective-permute-start = (bf16[1,8,128]{2,1,0:T(8,128)(2,1)}, bf16[1,8,128]{2,1,0:T(8,128)(2,1)S(1)}, u32[]{:S(2)}, u32[]{:S(2)}) collective-permute-start(bf16[1,8,128]{2,1,0:T(8,128)(2,1)} %bitcast.10), channel_id=1, source_target_pairs={{0,1},{1,0},{2,3},{3,2},{4,5},{5,4},{6,7},{7,6},{8,9},{9,8},{10,11... | collective-permute-start | bytes 6152 | tf_op jit(solution)/shard_map/ppermute | solution.py:133
  1.8 4.4 %collective-permute-start.1 = (bf16[2,8,128]{2,1,0:T(8,128)(2,1)S(1)}, bf16[2,8,128]{2,1,0:T(8,128)(2,1)S(1)}, u32[]{:S(2)}, u32[]{:S(2)}) collective-permute-start(bf16[2,8,128]{2,1,0:T(8,128)(2,1)S(1)} %pad_maximum_fusion.1.pair_ref.refs_0_), channel_id=1, source_target_pairs={{0,5},{1,4},{2,7},{3,6},{4,1},{5,0},{6,3},{7,2},{8,13},{9,12},{10,... | collective-permute-start | bytes 12296 | tf_op jit(solution)/shard_map/ppermute | solution.py:137
  4.5 3.5 %collective-permute-start.3 = (bf16[2,8,128]{2,1,0:T(8,128)(2,1)S(1)}, bf16[2,8,128]{2,1,0:T(8,128)(2,1)S(1)}, u32[]{:S(2)}, u32[]{:S(2)}) collective-permute-start(bf16[2,8,128]{2,1,0:T(8,128)(2,1)S(1)} %pad_maximum_fusion.1.pair_ref.refs_0_), channel_id=1, source_target_pairs={{0,3},{1,2},{2,1},{3,0},{4,7},{5,6},{6,5},{7,4},{8,11},{9,10},{10,... | collective-permute-start | bytes 12296 | tf_op jit(solution)/shard_map/ppermute | solution.py:133
  6.2 3.4 %collective-permute-start.2 = (bf16[4,8,128]{2,1,0:T(8,128)(2,1)S(1)}, bf16[4,8,128]{2,1,0:T(8,128)(2,1)S(1)}, u32[]{:S(2)}, u32[]{:S(2)}) collective-permute-start(bf16[4,8,128]{2,1,0:T(8,128)(2,1)S(1)} %shard_map.56), channel_id=1, source_target_pairs={{0,9},{1,8},{2,11},{3,10},{4,13},{5,12},{6,15},{7,14},{8,1},{9,0},... | collective-permute-start | bytes 24584 | tf_op jit(solution)/shard_map/ppermute | solution.py:137
  8.5 3.8 %collective-permute-start.5 = (f32[4,8,128]{2,1,0:T(8,128)S(1)}, f32[4,8,128]{2,1,0:T(8,128)S(1)}, u32[]{:S(2)}, u32[]{:S(2)}) collective-permute-start(f32[4,8,128]{2,1,0:T(8,128)S(1)} %get-tuple-element.31), channel_id=1, source_target_pairs={{0,8},{4,12},{8,0},{12,4},{16,24},{20,28},{24,16},{28,20},{1,9},{5... | collective-permute-start | bytes 49160 | tf_op jit(solution)/shard_map/ppermute | solution.py:133
  9.7 4.0 %collective-permute-start.4 = (bf16[4,8,128]{2,1,0:T(8,128)(2,1)S(1)}, bf16[4,8,128]{2,1,0:T(8,128)(2,1)S(1)}, u32[]{:S(2)}, u32[]{:S(2)}) collective-permute-start(bf16[4,8,128]{2,1,0:T(8,128)(2,1)S(1)} %pad_maximum_fusion), channel_id=1, source_target_pairs={{0,17},{1,16},{2,19},{3,18},{4,21},{5,20},{6,23},{7,22},{8,25},{9,... | collective-permute-start | bytes 24584 | tf_op jit(solution)/shard_map/ppermute | solution.py:137
  12.3 3.7 %collective-permute-start.7 = (f32[2,8,128]{2,1,0:T(8,128)S(1)}, f32[2,8,128]{2,1,0:T(8,128)S(1)}, u32[]{:S(2)}, u32[]{:S(2)}) collective-permute-start(f32[2,8,128]{2,1,0:T(8,128)S(1)} %slice.44), channel_id=1, source_target_pairs={{0,4},{4,0},{8,12},{12,8},{16,20},{20,16},{24,28},{28,24},{1,5},{5... | collective-permute-start | bytes 24584 | tf_op jit(solution)/shard_map/ppermute | solution.py:133
  14.3 4.3 %collective-permute-start.6 = (f32[2,8,128]{2,1,0:T(8,128)S(1)}, f32[2,8,128]{2,1,0:T(8,128)S(1)}, u32[]{:S(2)}, u32[]{:S(2)}) collective-permute-start(f32[2,8,128]{2,1,0:T(8,128)S(1)} %get-tuple-element.37), channel_id=1, source_target_pairs={{0,3},{1,2},{2,1},{3,0},{4,7},{5,6},{6,5},{7,4},{8,11},{9,10},{10,... | collective-permute-start | bytes 24584 | tf_op jit(solution)/shard_map/ppermute | solution.py:133
  16.0 4.5 %collective-permute-start.9 = (f32[1,8,128]{2,1,0:T(8,128)S(1)}, f32[1,8,128]{2,1,0:T(8,128)S(1)}, u32[]{:S(2)}, u32[]{:S(2)}) collective-permute-start(f32[1,8,128]{2,1,0:T(8,128)S(1)} %slice.45), channel_id=1, source_target_pairs={{0,16},{4,20},{8,24},{12,28},{16,0},{20,4},{24,8},{28,12},{1,17},{... | collective-permute-start | bytes 12296 | tf_op jit(solution)/shard_map/ppermute | solution.py:133
  18.6 1.9 %collective-permute-start.8 = (f32[1,8,128]{2,1,0:T(8,128)S(1)}, f32[1,8,128]{2,1,0:T(8,128)S(1)}, u32[]{:S(2)}, u32[]{:S(2)}) collective-permute-start(f32[1,8,128]{2,1,0:T(8,128)S(1)} %slice.47), channel_id=1, source_target_pairs={{0,1},{1,0},{2,3},{3,2},{4,5},{5,4},{6,7},{7,6},{8,9},{9,8},{10,11... | collective-permute-start | bytes 12296 | tf_op jit(solution)/shard_map/ppermute | solution.py:133

commit v4 on v0

--- a/solution.py
+++ b/solution.py
@@ -60,9 +60,8 @@
         pltpu.make_async_copy(tiles_ref.at[pl.ds(k * half, half)], stored_ref.at[pl.ds(k * half, half)], arrived.at[3 + k])
         for k in range(2)
     ]
-    for load in loads[:4]:
+    for load in loads:
         load.start()
-    loads[4].start(priority=1)
     for load in loads[:2]:
         load.wait()
     rows_axis, cols_axis = lax.axis_size("row"), lax.axis_size("col")

time: 21.3 us -> 21.3 us (level)
  no operation moved by 1% of the time
where the time goes in v4:
time: 21.3 us; the launch traced here: 21.1 us
  starting transfers between devices  14.8 us (69%)
  waiting for transfers between devices  2.55 us (12%)
  Pallas kernels  2.39 us (11%)
  between operations  0.72 us (3%)
  other arithmetic  0.62 us (3%)
    ppermute x7, starting transfers between devices, swapped(): lax.ppermute(x, axis, [(d, d ^ step) for d in range(lax.axis_size(axis))])  7.89 us
    ppermute x3, starting transfers between devices, crossing(): return lax.ppermute(x, ('row', 'col'), pairs)  6.93 us
    ppermute x7, waiting for transfers between devices, swapped(): lax.ppermute(x, axis, [(d, d ^ step) for d in range(lax.axis_size(axis))])  2.49 us
    pallas_call x1, Pallas kernels, per_device(): small_kernel(made_ready, [one_hot(slots, cols_axis), one_hot(rows_axis, s...  1.29 us
    pallas_call x2, Pallas kernels, terms(): small_kernel(functools.partial(slot_sums, contract), [half, half], [SCALA...  1.1 us
    add x1, other arithmetic, per_device(): row_terms[0] + row_in[0] + (col_terms[0] + after(col_in, row_terms)[0])  0.6 us
  transfers between devices with their start and end apart: 10, of which 4 were waited for; matrix products, arithmetic and copies ran while one was open for 0% of the time, Pallas kernels for 11%

profile of v4, /device:TPU:0, one launch (start us, length us, event | category | flops | bytes accessed | tf_op | source)
XLA Modules:
  0.0 21.1 jit_solution(7509771818220000746)
XLA Ops:
  0.0 0.5 %collective-permute-start = (bf16[1,8,128]{2,1,0:T(8,128)(2,1)}, bf16[1,8,128]{2,1,0:T(8,128)(2,1)S(1)}, u32[]{:S(2)}, u32[]{:S(2)}) collective-permute-start(bf16[1,8,128]{2,1,0:T(8,128)(2,1)} %bitcast.10), channel_id=1, source_target_pairs={{0,1},{1,0},{2,3},{3,2},{4,5},{5,4},{6,7},{7,6},{8,9},{9,8},{10,11... | collective-permute-start | bytes 6152 | tf_op jit(solution)/shard_map/ppermute | solution.py:131
  0.5 1.3 %shard_map.55 = (bf16[256,32]{1,0:T(8,128)(2,1)S(1)}, bf16[64,256]{1,0:T(8,128)(2,1)S(1)}, bf16[256,64]{1,0:T(8,128)(2,1)S(1)}, bf16[32,256]{1,0:T(8,128)(2,1)S(...) custom-call(s32[1,32]{1,0:T(1,128)} %bitcast.11, s32[1,32]{1,0:T(1,128)} %bitcast.12, ...), custom_call_target="tpu_custom_call" | custom-call | tf_op jit(solution)/shard_map/pallas_call | solution.py:153
  1.8 0.0 collective-permute-done
  1.8 2.7 %collective-permute-start.1 = (bf16[2,8,128]{2,1,0:T(8,128)(2,1)S(1)}, bf16[2,8,128]{2,1,0:T(8,128)(2,1)S(1)}, u32[]{:S(2)}, u32[]{:S(2)}) collective-permute-start(bf16[2,8,128]{2,1,0:T(8,128)(2,1)S(1)} %pad_maximum_fusion.1.pair_ref.refs_0_), channel_id=1, source_target_pairs={{0,5},{1,4},{2,7},{3,6},{4,1},{5,0},{6,3},{7,2},{8,13},{9,12},{10,... | collective-permute-start | bytes 12296 | tf_op jit(solution)/shard_map/ppermute | solution.py:135
  4.5 1.1 %collective-permute-start.3 = (bf16[2,8,128]{2,1,0:T(8,128)(2,1)S(1)}, bf16[2,8,128]{2,1,0:T(8,128)(2,1)S(1)}, u32[]{:S(2)}, u32[]{:S(2)}) collective-permute-start(bf16[2,8,128]{2,1,0:T(8,128)(2,1)S(1)} %pad_maximum_fusion.1.pair_ref.refs_0_), channel_id=1, source_target_pairs={{0,3},{1,2},{2,1},{3,0},{4,7},{5,6},{6,5},{7,4},{8,11},{9,10},{10,... | collective-permute-start | bytes 12296 | tf_op jit(solution)/shard_map/ppermute | solution.py:131
  6.2 0.0 collective-permute-done.1.new_ref
  6.2 1.8 %collective-permute-start.2 = (bf16[4,8,128]{2,1,0:T(8,128)(2,1)S(1)}, bf16[4,8,128]{2,1,0:T(8,128)(2,1)S(1)}, u32[]{:S(2)}, u32[]{:S(2)}) collective-permute-start(bf16[4,8,128]{2,1,0:T(8,128)(2,1)S(1)} %shard_map.56), channel_id=1, source_target_pairs={{0,9},{1,8},{2,11},{3,10},{4,13},{5,12},{6,15},{7,14},{8,1},{9,0},... | collective-permute-start | bytes 24584 | tf_op jit(solution)/shard_map/ppermute | solution.py:135
  8.0 0.0 collective-permute-done.3.refs_1_
  8.0 0.5 %shard_map.57 = (f32[4,8,128]{2,1,0:T(8,128)S(1)}, f32[4,8,128]{2,1,0:T(8,128)S(1)}) custom-call(s32[1,1]{1,0:T(1,128)S(6)} %copy.6.filled_ref, bf16[256,32]{1,0:T(8,128)(2,1)S(1)} %get-tuple-element.28.choice_ref, bf16[64,256]{1,0:T(8,128)(2,1)S(1)} %get-tuple-element.29.sums_ref, bf16[32,128,128]{2,1,0:T(8,128)(2,1)S(1)} %get-tuple-element.27.tiles_ref, ...), custom_call_target="tpu_custom_call" | custom-call | tf_op jit(solution)/shard_map/pallas_call | solution.py:148
  8.5 1.1 %collective-permute-start.5 = (f32[4,8,128]{2,1,0:T(8,128)S(1)}, f32[4,8,128]{2,1,0:T(8,128)S(1)}, u32[]{:S(2)}, u32[]{:S(2)}) collective-permute-start(f32[4,8,128]{2,1,0:T(8,128)S(1)} %get-tuple-element.31), channel_id=1, source_target_pairs={{0,8},{4,12},{8,0},{12,4},{16,24},{20,28},{24,16},{28,20},{1,9},{5... | collective-permute-start | bytes 49160 | tf_op jit(solution)/shard_map/ppermute | solution.py:131
  9.7 0.0 collective-permute-done.2
  9.7 2.5 %collective-permute-start.4 = (bf16[4,8,128]{2,1,0:T(8,128)(2,1)S(1)}, bf16[4,8,128]{2,1,0:T(8,128)(2,1)S(1)}, u32[]{:S(2)}, u32[]{:S(2)}) collective-permute-start(bf16[4,8,128]{2,1,0:T(8,128)(2,1)S(1)} %pad_maximum_fusion), channel_id=1, source_target_pairs={{0,17},{1,16},{2,19},{3,18},{4,21},{5,20},{6,23},{7,22},{8,25},{9,... | collective-permute-start | bytes 24584 | tf_op jit(solution)/shard_map/ppermute | solution.py:135
  12.2 0.2 collective-permute-done.5
  12.3 1.3 %collective-permute-start.7 = (f32[2,8,128]{2,1,0:T(8,128)S(1)}, f32[2,8,128]{2,1,0:T(8,128)S(1)}, u32[]{:S(2)}, u32[]{:S(2)}) collective-permute-start(f32[2,8,128]{2,1,0:T(8,128)S(1)} %slice.44), channel_id=1, source_target_pairs={{0,4},{4,0},{8,12},{12,8},{16,20},{20,16},{24,28},{28,24},{1,5},{5... | collective-permute-start | bytes 24584 | tf_op jit(solution)/shard_map/ppermute | solution.py:131
  13.7 0.1 collective-permute-done.4.refs_3_
  13.7 0.6 %shard_map.58 = (f32[2,8,128]{2,1,0:T(8,128)S(1)}, f32[2,8,128]{2,1,0:T(8,128)S(1)}) custom-call(s32[1,1]{1,0:T(1,128)S(6)} %copy.6.filled_ref, bf16[256,64]{1,0:T(8,128)(2,1)S(1)} %get-tuple-element.25.choice_ref, bf16[32,256]{1,0:T(8,128)(2,1)S(1)} %get-tuple-element.26.sums_ref, bf16[32,128,128]{2,1,0:T(8,128)(2,1)S(1)} %get-tuple-element.27.tiles_ref, ...), custom_call_target="tpu_custom_call" | custom-call | tf_op jit(solution)/shard_map/pallas_call | solution.py:148
  14.3 1.2 %collective-permute-start.6 = (f32[2,8,128]{2,1,0:T(8,128)S(1)}, f32[2,8,128]{2,1,0:T(8,128)S(1)}, u32[]{:S(2)}, u32[]{:S(2)}) collective-permute-start(f32[2,8,128]{2,1,0:T(8,128)S(1)} %get-tuple-element.37), channel_id=1, source_target_pairs={{0,3},{1,2},{2,1},{3,0},{4,7},{5,6},{6,5},{7,4},{8,11},{9,10},{10,... | collective-permute-start | bytes 24584 | tf_op jit(solution)/shard_map/ppermute | solution.py:131
  15.5 0.5 %collective-permute-done.7 = f32[2,8,128]{2,1,0:T(8,128)S(1)} collective-permute-done((f32[2,8,128]{2,1,0:T(8,128)S(1)}, f32[2,8,128]{2,1,0:T(8,128)S(1)}, u32[]{:S(2)}, u32[]{:S(2)}) %collective-permute-start.7) | collective-permute-done | bytes 8224 | tf_op jit(solution)/shard_map/ppermute | solution.py:131
  16.0 2.6 %collective-permute-start.9 = (f32[1,8,128]{2,1,0:T(8,128)S(1)}, f32[1,8,128]{2,1,0:T(8,128)S(1)}, u32[]{:S(2)}, u32[]{:S(2)}) collective-permute-start(f32[1,8,128]{2,1,0:T(8,128)S(1)} %slice.45), channel_id=1, source_target_pairs={{0,16},{4,20},{8,24},{12,28},{16,0},{20,4},{24,8},{28,12},{1,17},{... | collective-permute-start | bytes 12296 | tf_op jit(solution)/shard_map/ppermute | solution.py:131
  18.6 0.0 collective-permute-done.6
  18.6 0.1 collective-permute-start.8
  18.7 1.8 %collective-permute-done.9 = f32[1,8,128]{2,1,0:T(8,128)S(1)} collective-permute-done((f32[1,8,128]{2,1,0:T(8,128)S(1)}, f32[1,8,128]{2,1,0:T(8,128)S(1)}, u32[]{:S(2)}, u32[]{:S(2)}) %collective-permute-start.9) | collective-permute-done | bytes 4128 | tf_op jit(solution)/shard_map/ppermute | solution.py:131
  20.5 0.0 collective-permute-done.8
  20.5 0.6 %fusion.1 = f32[8,128]{1,0:T(8,128)} fusion(f32[1,8,128]{2,1,0:T(8,128)S(1)} %collective-permute-done.9, f32[2,8,128]{2,1,0:T(8,128)S(1)} %slice_add_fusion, f32[1,8,128]{2,1,0:T(8,128)S(1)} %collective-permute-done.8, f32[2,8,128]{2,1,0:T(8,128)S(1)} %add.25), kind=kLoop, calls=%fused_computation.4 | loop fusion | flops 3072 | bytes 20480 | tf_op jit(solution)/shard_map/add | solution.py:203
  (11 shorter events, 0.0 us)
Async XLA Ops:
  0.0 1.8 %collective-permute-start = (bf16[1,8,128]{2,1,0:T(8,128)(2,1)}, bf16[1,8,128]{2,1,0:T(8,128)(2,1)S(1)}, u32[]{:S(2)}, u32[]{:S(2)}) collective-permute-start(bf16[1,8,128]{2,1,0:T(8,128)(2,1)} %bitcast.10), channel_id=1, source_target_pairs={{0,1},{1,0},{2,3},{3,2},{4,5},{5,4},{6,7},{7,6},{8,9},{9,8},{10,11... | collective-permute-start | bytes 6152 | tf_op jit(solution)/shard_map/ppermute | solution.py:131
  1.8 4.4 %collective-permute-start.1 = (bf16[2,8,128]{2,1,0:T(8,128)(2,1)S(1)}, bf16[2,8,128]{2,1,0:T(8,128)(2,1)S(1)}, u32[]{:S(2)}, u32[]{:S(2)}) collective-permute-start(bf16[2,8,128]{2,1,0:T(8,128)(2,1)S(1)} %pad_maximum_fusion.1.pair_ref.refs_0_), channel_id=1, source_target_pairs={{0,5},{1,4},{2,7},{3,6},{4,1},{5,0},{6,3},{7,2},{8,13},{9,12},{10,... | collective-permute-start | bytes 12296 | tf_op jit(solution)/shard_map/ppermute | solution.py:135
  4.5 3.5 %collective-permute-start.3 = (bf16[2,8,128]{2,1,0:T(8,128)(2,1)S(1)}, bf16[2,8,128]{2,1,0:T(8,128)(2,1)S(1)}, u32[]{:S(2)}, u32[]{:S(2)}) collective-permute-start(bf16[2,8,128]{2,1,0:T(8,128)(2,1)S(1)} %pad_maximum_fusion.1.pair_ref.refs_0_), channel_id=1, source_target_pairs={{0,3},{1,2},{2,1},{3,0},{4,7},{5,6},{6,5},{7,4},{8,11},{9,10},{10,... | collective-permute-start | bytes 12296 | tf_op jit(solution)/shard_map/ppermute | solution.py:131
  6.2 3.4 %collective-permute-start.2 = (bf16[4,8,128]{2,1,0:T(8,128)(2,1)S(1)}, bf16[4,8,128]{2,1,0:T(8,128)(2,1)S(1)}, u32[]{:S(2)}, u32[]{:S(2)}) collective-permute-start(bf16[4,8,128]{2,1,0:T(8,128)(2,1)S(1)} %shard_map.56), channel_id=1, source_target_pairs={{0,9},{1,8},{2,11},{3,10},{4,13},{5,12},{6,15},{7,14},{8,1},{9,0},... | collective-permute-start | bytes 24584 | tf_op jit(solution)/shard_map/ppermute | solution.py:135
  8.5 3.8 %collective-permute-start.5 = (f32[4,8,128]{2,1,0:T(8,128)S(1)}, f32[4,8,128]{2,1,0:T(8,128)S(1)}, u32[]{:S(2)}, u32[]{:S(2)}) collective-permute-start(f32[4,8,128]{2,1,0:T(8,128)S(1)} %get-tuple-element.31), channel_id=1, source_target_pairs={{0,8},{4,12},{8,0},{12,4},{16,24},{20,28},{24,16},{28,20},{1,9},{5... | collective-permute-start | bytes 49160 | tf_op jit(solution)/shard_map/ppermute | solution.py:131
  9.7 4.0 %collective-permute-start.4 = (bf16[4,8,128]{2,1,0:T(8,128)(2,1)S(1)}, bf16[4,8,128]{2,1,0:T(8,128)(2,1)S(1)}, u32[]{:S(2)}, u32[]{:S(2)}) collective-permute-start(bf16[4,8,128]{2,1,0:T(8,128)(2,1)S(1)} %pad_maximum_fusion), channel_id=1, source_target_pairs={{0,17},{1,16},{2,19},{3,18},{4,21},{5,20},{6,23},{7,22},{8,25},{9,... | collective-permute-start | bytes 24584 | tf_op jit(solution)/shard_map/ppermute | solution.py:135
  12.3 3.7 %collective-permute-start.7 = (f32[2,8,128]{2,1,0:T(8,128)S(1)}, f32[2,8,128]{2,1,0:T(8,128)S(1)}, u32[]{:S(2)}, u32[]{:S(2)}) collective-permute-start(f32[2,8,128]{2,1,0:T(8,128)S(1)} %slice.44), channel_id=1, source_target_pairs={{0,4},{4,0},{8,12},{12,8},{16,20},{20,16},{24,28},{28,24},{1,5},{5... | collective-permute-start | bytes 24584 | tf_op jit(solution)/shard_map/ppermute | solution.py:131
  14.3 4.3 %collective-permute-start.6 = (f32[2,8,128]{2,1,0:T(8,128)S(1)}, f32[2,8,128]{2,1,0:T(8,128)S(1)}, u32[]{:S(2)}, u32[]{:S(2)}) collective-permute-start(f32[2,8,128]{2,1,0:T(8,128)S(1)} %get-tuple-element.37), channel_id=1, source_target_pairs={{0,3},{1,2},{2,1},{3,0},{4,7},{5,6},{6,5},{7,4},{8,11},{9,10},{10,... | collective-permute-start | bytes 24584 | tf_op jit(solution)/shard_map/ppermute | solution.py:131
  16.0 4.5 %collective-permute-start.9 = (f32[1,8,128]{2,1,0:T(8,128)S(1)}, f32[1,8,128]{2,1,0:T(8,128)S(1)}, u32[]{:S(2)}, u32[]{:S(2)}) collective-permute-start(f32[1,8,128]{2,1,0:T(8,128)S(1)} %slice.45), channel_id=1, source_target_pairs={{0,16},{4,20},{8,24},{12,28},{16,0},{20,4},{24,8},{28,12},{1,17},{... | collective-permute-start | bytes 12296 | tf_op jit(solution)/shard_map/ppermute | solution.py:131
  18.6 1.9 %collective-permute-start.8 = (f32[1,8,128]{2,1,0:T(8,128)S(1)}, f32[1,8,128]{2,1,0:T(8,128)S(1)}, u32[]{:S(2)}, u32[]{:S(2)}) collective-permute-start(f32[1,8,128]{2,1,0:T(8,128)S(1)} %slice.47), channel_id=1, source_target_pairs={{0,1},{1,0},{2,3},{3,2},{4,5},{5,4},{6,7},{7,6},{8,9},{9,8},{10,11... | collective-permute-start | bytes 12296 | tf_op jit(solution)/shard_map/ppermute | solution.py:131
